TPU v7x, 256 devices: a whole 4x4x8 slice. The times are simulated.
256 devices in a mesh: seq: 64 (over y, z, core), mp: 4 (over x).
Axes of the slice: x: 4, y: 4, z: 8, core: 2. Of those that a mesh axis runs over, the one named last changes fastest.
Arguments:
- phoneme_rows: bfloat16 [8192, 1024], P('seq'), may hold values from -6 to 6
- durations: int32 [8192], P('seq'), may hold values from 1 to 40, as said below
- conv_first: bfloat16 [3, 1024, 512], P(None, None, 'mp'), may hold values from -0.109375 to 0.109375
- conv_second: bfloat16 [2, 3, 256, 256], replicated, may hold values from -0.21875 to 0.21875
- readout: bfloat16 [2, 256], replicated, may hold values from -0.375 to 0.375
- targets: float32 [2, 65536], P(None, 'seq'), may hold values from -6 to 6
Outputs:
- predicted: float32 [2, 65536], P(None, 'seq')
- row_grad: bfloat16 [8192, 1024], P('seq', 'mp')
Inputs may be any that keep to these rules, and one draw needn't show every extreme that they name: The durations sum to 65536. In every aligned block of 128 phonemes one phoneme lasts 40 frames and another 1 frame. Every frame from d * 1024 - 2 to (d + 1) * 1024 + 1 that lies in the window belongs to a phoneme of seq indices d - 2 to d + 2, and in every draw some frames need phonemes 2 indices away.
All inputs are finite; a program needn't handle non-finite values.
Results may differ from a plain program's by a relative error of at most 0.015.
Values may be sent and summed in bfloat16 or wider, within the bound.
No kernel may reach another device: no remote copies, remote signals or barrier semaphores. Data moves between devices by JAX's collectives and lax.ppermute only.
A program may use at most 64 MiB of HBM per device.

v0:
```python
import functools

import jax
import jax.numpy as jnp
from jax import lax
from jax.experimental import pallas as pl
from jax.experimental.pallas import tpu as pltpu
from jax.sharding import PartitionSpec as P

EPSILON = 1e-05
TILE = 512
STRIDE = 508
LEAD = 3
HALO = 4
EDGE = 16
LONGEST = 40
REACH = 2
NEAR = 1
f32 = jnp.float32
bf16 = jnp.bfloat16
VMEM = pltpu.VMEM
SMEM = pltpu.SMEM


def whole():
    return pl.BlockSpec(memory_space=VMEM)


def copied(shape):
    return pl.BlockSpec(shape, lambda _: (0,) * len(shape))


def in_hbm(array):
    return pltpu.with_memory_space_constraint(array, pltpu.HBM)


def scalars():
    return pl.BlockSpec(memory_space=SMEM)


def call(kernel, name, *, flops=0, moved=0, vmem=24, **kwargs):
    return pl.pallas_call(
        kernel,
        name=name,
        grid=(1,),
        cost_estimate=pl.CostEstimate(flops=flops, bytes_accessed=moved, transcendentals=0),
        compiler_params=pltpu.CompilerParams(vmem_limit_bytes=vmem * 1024 * 1024),
        **kwargs,
    )


def rotate(block, axis, distance):
    size = lax.axis_size(axis)
    return lax.ppermute(block, axis, [(i, (i + distance) % size) for i in range(size)])


def pack_kernel(where_ref, dur_ref, targets_ref, readout_ref, head_ref, tail_ref, to_mate_ref, to_outer_ref):
    block = dur_ref.shape[1]
    frames = targets_ref.shape[1]
    channels = readout_ref.shape[1]
    even = jnp.bitwise_and(where_ref[0], 1) == 0
    tail = tail_ref[...].astype(f32)[16 - HALO : 16]
    head = head_ref[...].astype(f32)[0:HALO]
    rows = (jnp.where(even, tail, head), jnp.where(even, head, tail))
    readout = readout_ref[...].astype(f32)
    for out, halo in zip((to_mate_ref, to_outer_ref), rows):
        out[...] = jnp.zeros_like(out)
        out[0:2, 0:frames] = targets_ref[...]
        out[2:3, 0:block] = dur_ref[...].astype(f32)
        for q in range(2):
            out[3:4, q * channels : (q + 1) * channels] = readout[q : q + 1]
        out[HALO : 2 * HALO, :] = halo


def prepare_kernel(where_ref, dur_ref, rows_ref, conv_ref, second_ref, spread_ref, products_ref, *refs):
    bundle_refs, (turned_ref, wide_ref, sem) = refs[:4], refs[4:]
    wide_ref[...] = jnp.broadcast_to(dur_ref[...], wide_ref.shape)
    spread = pltpu.make_async_copy(wide_ref, spread_ref, sem)
    spread.start()
    taps, width, _ = conv_ref.shape
    block = rows_ref.shape[0]
    channels = second_ref.shape[2]
    members = len(bundle_refs)
    features = width // members
    low = taps * (block // members + 2 * EDGE)
    for k in range(taps):
        product = jnp.dot(rows_ref[...], conv_ref[k], preferred_element_type=f32)
        products_ref[k * block : (k + 1) * block, :] = product.astype(bf16)
    for d in range(members):
        target = lax.rem(where_ref[1] + d, members)
        at = pl.ds(pl.multiple_of(target * features, features), features)
        for k in range(taps):
            bundle_refs[d][low + k * features : low + (k + 1) * features, :] = conv_ref[k, at, :]
    for q in range(2):
        for k in range(taps):
            turned_ref[q, :, k * channels : (k + 1) * channels] = second_ref[q, k].T
    spread.wait()


def split(values):
    terms = []
    for _ in range(3):
        terms.append(values.astype(bf16).astype(f32))
        values = values - terms[-1]
    return terms


def pieces_kernel(where_ref, products_ref, mate_ref, outer_ref, far_ref, *refs):
    given_refs, bundle_refs, (left_ref, right_ref, halo_ref, table_ref) = refs[:4], refs[4:8], refs[8:]
    even = jnp.bitwise_and(where_ref[0], 1) == 0
    left_ref[...] = jnp.where(even, outer_ref[...], mate_ref[...])
    right_ref[...] = jnp.where(even, mate_ref[...], outer_ref[...])
    channels = products_ref.shape[1]
    members = len(bundle_refs)
    features = halo_ref.shape[1] // members
    taps = table_ref.shape[0]
    block = products_ref.shape[0] // taps
    share = block // members
    window = share + 2 * EDGE
    low = taps * window
    high = low + taps * features
    halo_ref[...] = jnp.zeros_like(halo_ref)
    halo_ref[EDGE - HALO : EDGE, :] = left_ref[HALO : 2 * HALO]
    halo_ref[EDGE : EDGE + HALO, :] = right_ref[HALO : 2 * HALO]
    for k in range(taps):
        product = jnp.zeros((2 * EDGE, channels), f32)
        for d in range(members):
            owner = lax.rem(where_ref[1] + d, members)
            part = halo_ref[:, pl.ds(pl.multiple_of(owner * features, features), features)].astype(bf16)
            cut = given_refs[d][low + k * features : low + (k + 1) * features, :]
            product = product + jnp.dot(part, cut, preferred_element_type=f32)
        table_ref[k, 0:EDGE, :] = product[0:EDGE].astype(bf16)
        table_ref[k, EDGE : EDGE + block, :] = products_ref[k * block : (k + 1) * block, :]
        table_ref[k, EDGE + block :, :] = product[EDGE:].astype(bf16)
    far = far_ref[...]
    parts = [
        term[:, c * channels : (c + 1) * channels]
        for term in split(far)
        for c in range(far.shape[1] // channels)
    ]
    parts = jnp.concatenate(parts, axis=0).astype(bf16)
    for d in range(members):
        target = lax.rem(where_ref[1] + d, members)
        at = pl.ds(pl.multiple_of(target * share, share), window)
        for k in range(taps):
            bundle_refs[d][k * window : (k + 1) * window, :] = table_ref[k, at, :]
        bundle_refs[d][high:, :] = parts


def share_bounds(where_ref, own_ref, left_ref, right_ref, last_seq, rows, first_row):
    block = 4 * (rows - 2 * (EDGE - first_row))
    share = block // 4
    s, m = where_ref[0], where_ref[1]
    lane = lax.broadcasted_iota(jnp.int32, (1, block), 1)
    near = jnp.where((lane >= block - HALO) & (s > 0), left_ref[2:3, 0:block], 0.0)
    far = jnp.where((lane < HALO) & (s < last_seq), right_ref[2:3, 0:block], 0.0)
    own = own_ref[2:3, 0:block]
    durations = jnp.concatenate([near, own, far], axis=1)
    phoneme = lax.broadcasted_iota(jnp.int32, (1, 3 * block), 1) - block
    begin = m * share
    row = lax.broadcasted_iota(jnp.int32, (rows, 3 * block), 0) + (begin + first_row - EDGE)
    at = jnp.broadcast_to(phoneme, (rows, 3 * block))
    spread = jnp.broadcast_to(durations, (rows, 3 * block))
    later = at >= begin

    def bound(limit):
        signed = jnp.where(later & (at < limit), spread, 0.0) - jnp.where(
            (at < begin) & (at >= limit), spread, 0.0
        )
        return jnp.sum(signed, axis=1, keepdims=True)

    count = jnp.sum(jnp.where((phoneme >= begin) & (phoneme < begin + share), durations, 0.0))
    skipped = jnp.sum(jnp.where((phoneme >= 0) & (phoneme < begin), durations, 0.0))
    return bound(row), bound(row + 1), count, skipped, jnp.sum(own)


def tiles_of(count):
    return lax.div(count.astype(jnp.int32) + (2 + STRIDE - 1), STRIDE)


def one_hot(frames, starts, ends):
    return jnp.where((frames >= starts) & (frames < ends), 1.0, 0.0).astype(bf16)


def local_frames(t):
    lane = lax.broadcasted_iota(jnp.int32, (1, TILE), 1)
    return (lane + (t * STRIDE - LEAD)).astype(f32), lane


def column_mean(values):
    return jnp.sum(values, axis=0, keepdims=True) * (1.0 / values.shape[0])


def with_neighbours(values):
    return jnp.concatenate(
        [
            pltpu.roll(values, 1, 1).astype(bf16),
            values.astype(bf16),
            pltpu.roll(values, TILE - 1, 1).astype(bf16),
        ],
        axis=0,
    )


def forward_kernel(
    last_seq,
    where_ref,
    own_ref,
    left_ref,
    right_ref,
    piece_ref,
    one_ref,
    two_ref,
    three_ref,
    kernel_ref,
    pred_ref,
    offset_ref,
    near_ref,
    far_kept_ref,
    bounds_ref,
    table_ref,
    weight_ref,
    more_ref,
    sems,
):
    channels = kernel_ref.shape[1]
    chunk = piece_ref.shape[1]
    taps = kernel_ref.shape[2] // channels
    window = bounds_ref.shape[1]
    depth = taps * window
    members = 2 * channels // chunk
    s, m = where_ref[0], where_ref[1]
    starts, ends, total, skipped, block_total = share_bounds(
        where_ref, own_ref, left_ref, right_ref, last_seq, window, 0
    )
    bounds_ref[0] = jnp.broadcast_to(starts, (window, TILE))
    bounds_ref[1] = jnp.broadcast_to(ends, (window, TILE))
    lowest = jnp.where(s == 0, -skipped, -1e9)
    end = jnp.where(s == last_seq, block_total - skipped, 1e9)
    for q in range(2):
        column = own_ref[:, q * channels : (q + 1) * channels].T
        weight_ref[q] = jnp.broadcast_to(column[:, 3:4], (channels, TILE))
    for d, source in enumerate((piece_ref, one_ref, two_ref, three_ref)):
        owner = lax.rem(m + members - d, members)
        table_ref[pl.ds(pl.multiple_of(owner * chunk, chunk), chunk), :] = source[0:depth, :].T

    for q in range(2):
        column = own_ref[:, q * channels : (q + 1) * channels].T
        weight_ref[q] = jnp.broadcast_to(column[:, 3:4], (channels, TILE))
    offset_ref[0] = skipped.astype(jnp.int32)
    offset_ref[1] = total.astype(jnp.int32)
    pred_ref[...] = jnp.zeros_like(pred_ref)

    def work(t, kept_ref, at):
        frames, lane = local_frames(t)
        selector = jnp.concatenate(
            [one_hot(frames + (k - 1.0), bounds_ref[0], bounds_ref[1]) for k in range(taps)], axis=0
        )
        inside = jnp.where((frames >= lowest) & (frames < end), 1.0, 0.0)
        answered = jnp.where((lane >= 2) & (lane < 2 + STRIDE), inside, 0.0)
        for q in range(2):
            low, high = q * channels, (q + 1) * channels
            first = jnp.dot(table_ref[low:high, :], selector, preferred_element_type=f32)
            act = (jnp.maximum(first, 0.0) + jnp.log(1.0 + jnp.exp(-jnp.abs(first)))).astype(bf16).astype(f32)
            centered = act - column_mean(act)
            inverse_one = lax.rsqrt(column_mean(centered * centered) + EPSILON)
            hidden = centered * (inverse_one * inside)
            kept_ref[at, q, 2] = ((1.0 - jnp.exp(-act)) * (inverse_one * answered)).astype(bf16)
            stacked = with_neighbours(hidden)
            kept_ref[at, q, 0] = stacked[channels : 2 * channels]
            second = jnp.dot(kernel_ref[q], stacked, preferred_element_type=f32)
            small = jnp.exp(-jnp.abs(second))
            soft = jnp.maximum(second, 0.0) + jnp.log(1.0 + small)
            sigmoid = jnp.exp(second - soft)
            centered = soft - column_mean(soft)
            inverse_two = lax.rsqrt(column_mean(centered * centered) + EPSILON)
            normed = centered * inverse_two
            weights = weight_ref[q]
            weighted_mean = column_mean(normed * weights)
            pred_ref[t, q : q + 1, :] = weighted_mean * float(channels)
            factor = (weights - column_mean(weights) - normed * weighted_mean) * sigmoid
            kept_ref[at, q, 1] = (factor * (inverse_two * inside)).astype(bf16)

    def step(t, carry):
        work(t, near_ref, t)
        return carry

    def far_step(t, carry):
        work(t, more_ref, t - NEAR)
        pltpu.make_async_copy(more_ref.at[t - NEAR], far_kept_ref.at[t - NEAR], sems.at[t - NEAR]).start()
        return carry

    def wait(t, carry):
        pltpu.make_async_copy(more_ref.at[t - NEAR], far_kept_ref.at[t - NEAR], sems.at[t - NEAR]).wait()
        return carry

    tiles = tiles_of(total)
    lax.fori_loop(0, jnp.minimum(tiles, NEAR), step, 0)
    lax.fori_loop(NEAR, tiles, far_step, 0)
    lax.fori_loop(NEAR, tiles, wait, 0)


def align_kernel(
    where_ref,
    offset_ref,
    spread_ref,
    pred_ref,
    own_ref,
    left_ref,
    right_ref,
    far_ref,
    one_ref,
    far_kept_ref,
    residual_ref,
    kept_ref,
    *refs,
):
    slot_refs, (window_ref, placed_ref, sems) = refs[:5], refs[5:]
    s, m = where_ref[0], where_ref[1]
    chunk = one_ref.shape[1]
    frames_each = far_ref.shape[1]
    count = offset_ref[1]
    tiles = lax.div(count + (2 + STRIDE - 1), STRIDE)

    def fetch(t, carry):
        pltpu.make_async_copy(far_kept_ref.at[t - NEAR], kept_ref.at[t - NEAR], sems.at[t - NEAR]).start()
        return carry

    def wait(t, carry):
        pltpu.make_async_copy(far_kept_ref.at[t - NEAR], kept_ref.at[t - NEAR], sems.at[t - NEAR]).wait()
        return carry

    lax.fori_loop(NEAR, tiles, fetch, 0)
    seq = lax.broadcasted_iota(jnp.int32, spread_ref.shape, 0)
    before = jnp.sum(jnp.where(seq < s, spread_ref[...].astype(f32), 0.0))
    offset = before.astype(jnp.int32) + offset_ref[0] - (s - REACH) * frames_each
    window_ref[...] = jnp.zeros_like(window_ref)
    placed_ref[...] = jnp.zeros_like(placed_ref)
    parts = one_ref[one_ref.shape[0] - 3 * 2 * frames_each // chunk :, :].astype(f32)
    terms = [parts[i * 2 * frames_each // chunk : (i + 1) * 2 * frames_each // chunk] for i in range(3)]
    terms = terms[0] + terms[1] + terms[2]
    other = jnp.concatenate([terms[2 * c : 2 * c + 2] for c in range(frames_each // chunk)], axis=1)
    even = jnp.bitwise_and(m, 1) == 0
    here = far_ref[...]
    beside = (jnp.where(even, here, other), left_ref[0:2], own_ref[0:2], right_ref[0:2], jnp.where(even, other, here))
    for i, source in enumerate(beside):
        window_ref[0:2, TILE + i * frames_each : TILE + (i + 1) * frames_each] = source
    exact_lane = lax.broadcasted_iota(jnp.int32, (2, TILE), 1)
    exact = (exact_lane >= LEAD) & (exact_lane < LEAD + STRIDE)

    def step(t, carry):
        at = jnp.clip(TILE + offset + t * STRIDE - LEAD, 0, window_ref.shape[1] - TILE - 128)
        rest = jnp.bitwise_and(at, 127)
        near = pl.ds(pl.multiple_of(at - rest, 128), TILE + 128)
        taken = pltpu.roll(window_ref[:, near], TILE + 128 - rest, 1)[0:2, 0:TILE]
        values = pred_ref[t]
        residual_ref[t] = values - taken
        own = exact & (exact_lane + (t * STRIDE - LEAD) < count)
        moved = jnp.concatenate([jnp.where(own, values, 0.0), jnp.zeros((2, 128), f32)], axis=1)
        moved = jnp.concatenate([moved, jnp.zeros((6, TILE + 128), f32)], axis=0)
        placed_ref[:, near] = placed_ref[:, near] + pltpu.roll(moved, rest, 1)
        return carry

    lax.fori_loop(0, tiles, step, 0)
    even = jnp.bitwise_and(s, 1) == 0
    slots = [placed_ref[0:2, TILE + i * frames_each : TILE + (i + 1) * frames_each] for i in range(5)]
    slots[1], slots[3] = jnp.where(even, slots[1], slots[3]), jnp.where(even, slots[3], slots[1])
    for slot, values in zip(slot_refs, slots):
        slot[...] = values
    lax.fori_loop(NEAR, tiles, wait, 0)


def backward_kernel(
    last_seq,
    where_ref,
    own_ref,
    left_ref,
    right_ref,
    residual_ref,
    near_ref,
    more_ref,
    turned_ref,
    out_ref,
    bounds_ref,
    sums_ref,
    conv_ref,
):
    taps = conv_ref.shape[1]
    channels = conv_ref.shape[2]
    share = bounds_ref.shape[1]
    starts, ends, count, _, _ = share_bounds(where_ref, own_ref, left_ref, right_ref, last_seq, share, EDGE)
    bounds_ref[0] = jnp.broadcast_to(starts, (share, TILE))
    bounds_ref[1] = jnp.broadcast_to(ends, (share, TILE))
    sums_ref[...] = jnp.zeros_like(sums_ref)
    for q in range(2):
        for k in range(taps):
            conv_ref[q, k] = turned_ref[q, :, k * channels : (k + 1) * channels].T

    def work(t, kept_ref, at):
        frames, _ = local_frames(t)
        selector = jnp.concatenate(
            [one_hot(frames + (k - 1.0), bounds_ref[0], bounds_ref[1]) for k in range(taps)], axis=0
        )
        for q in range(2):
            low, high = q * channels, (q + 1) * channels
            grad_second = kept_ref[at, q, 1].astype(f32) * residual_ref[t, q : q + 1, :]
            stacked = with_neighbours(grad_second)
            grad_hidden = jnp.zeros((channels, TILE), f32)
            for k in range(taps):
                part = stacked[(taps - 1 - k) * channels : (taps - k) * channels]
                grad_hidden = grad_hidden + jnp.dot(conv_ref[q, k], part, preferred_element_type=f32)
            normed = kept_ref[at, q, 0].astype(f32)
            first_mean = column_mean(grad_hidden)
            second_mean = column_mean(grad_hidden * normed)
            scale = kept_ref[at, q, 2].astype(f32)
            grad_first = (grad_hidden - first_mean - normed * second_mean) * scale
            sums_ref[:, low:high] += lax.dot_general(
                selector, grad_first.astype(bf16), (((1,), (1,)), ((), ())), preferred_element_type=f32
            )

    def step(t, carry):
        work(t, near_ref, t)
        return carry

    def far_step(t, carry):
        work(t, more_ref, t - NEAR)
        return carry

    tiles = tiles_of(count)
    lax.fori_loop(0, jnp.minimum(tiles, NEAR), step, 0)
    lax.fori_loop(NEAR, tiles, far_step, 0)
    out_ref[...] = sums_ref[...].astype(bf16)


def merge_kernel(sums_ref, own_ref, *refs):
    arrived, out_ref = refs[:-1], refs[-1]
    depth = sums_ref.shape[0]
    half = out_ref.shape[1]
    out_ref[0:depth, :] = sums_ref[...]
    left = own_ref[...]
    for source in arrived:
        left = left + source[...]
    parts = [term[:, i * half : (i + 1) * half] for term in split(left) for i in range(2)]
    parts.append(jnp.zeros((4, half), f32))
    out_ref[depth:, :] = jnp.concatenate(parts, axis=0).astype(bf16)


def finish_kernel(where_ref, *refs):
    merged_refs, bundle_refs, (pred_ref, out_ref, rows_ref) = refs[:4], refs[4:8], refs[8:]
    taps = rows_ref.shape[0]
    chunk = bundle_refs[0].shape[1]
    features = out_ref.shape[1]
    members = len(merged_refs)
    low = taps * (rows_ref.shape[1] // members + 2 * EDGE)
    share = rows_ref.shape[1] // members
    depth = taps * share
    half = merged_refs[0].shape[1]
    pred = jnp.zeros((2, 2 * half), f32)
    for d, source in enumerate(merged_refs):
        owner = lax.rem(where_ref[1] + members - d, members)
        at = pl.ds(pl.multiple_of(owner * share, share), share)
        for k in range(taps):
            rows_ref[k, at, :] = source[k * share : (k + 1) * share, :]
        parts = source[depth:, :].astype(f32)
        for i in range(3):
            pred = pred + jnp.concatenate([parts[4 * i : 4 * i + 2], parts[4 * i + 2 : 4 * i + 4]], axis=1)
    pred_ref[...] = pred
    total = jnp.zeros(out_ref.shape, f32)
    for pair in (0, 2):
        owners = [lax.rem(where_ref[1] + members - d, members) for d in (pair, pair + 1)]
        sources = bundle_refs[pair : pair + 2]
        for k in range(taps):
            rows = [rows_ref[k, :, pl.ds(pl.multiple_of(owner * chunk, chunk), chunk)] for owner in owners]
            cuts = [source[low + k * features : low + (k + 1) * features, :] for source in sources]
            total = total + lax.dot_general(
                jnp.concatenate(rows, axis=1),
                jnp.concatenate(cuts, axis=1),
                (((1,), (1,)), ((), ())),
                preferred_element_type=f32,
            )
    out_ref[...] = total.astype(bf16)


def body(phoneme_rows, durations, conv_first, conv_second, readout, targets):
    seq_size = lax.axis_size("seq")
    members = lax.axis_size("mp")
    block, width = phoneme_rows.shape
    frames = targets.shape[1]
    taps, _, chunk = conv_first.shape
    channels = conv_second.shape[2]
    features = width // members
    share = block // members
    window = share + 2 * EDGE
    most = -(-(share * LONGEST + 2) // STRIDE)
    last_seq = seq_size - 1
    where = jnp.stack([lax.axis_index("seq"), lax.axis_index("mp")]).astype(jnp.int32)
    anywhere = pl.BlockSpec(memory_space=pl.ANY)
    pack = jax.ShapeDtypeStruct((2 * HALO, width), f32)
    dur = durations.reshape(1, block)

    to_mate, to_outer = call(
        pack_kernel,
        "pack",
        vmem=4,
        moved=2 * 32 * width,
        out_shape=(pack, pack),
        in_specs=[
            scalars(),
            copied((1, block)),
            copied(targets.shape),
            copied(readout.shape),
            pl.BlockSpec((16, width), lambda _: (0, 0)),
            pl.BlockSpec((16, width), lambda _: (block // 16 - 1, 0)),
        ],
        out_specs=(whole(),) * 2,
    )(where, in_hbm(dur), in_hbm(targets), in_hbm(readout), in_hbm(phoneme_rows), in_hbm(phoneme_rows))

    def outer_of(s):
        return (s + (1 if s % 2 else -1)) % seq_size

    from_mate = lax.ppermute(to_mate, "seq", [(s, s ^ 1) for s in range(seq_size)])
    from_outer = lax.ppermute(to_outer, "seq", [(s, outer_of(s)) for s in range(seq_size)])
    far = lax.ppermute(
        targets,
        ("seq", "mp"),
        [
            ((s + (-REACH if m % 2 == 0 else REACH)) % seq_size * members + m, s * members + m)
            for s in range(seq_size)
            for m in range(members)
        ],
    )

    bundle = jax.ShapeDtypeStruct((taps * (window + features) + 3 * 2 * frames // chunk, chunk), bf16)
    spread, products, *made = call(
        prepare_kernel,
        "prepare",
        vmem=12,
        flops=2 * block * width * taps * chunk,
        moved=2 * block * width + 2 * taps * width * chunk + 4 * taps * channels * channels,
        out_shape=(pltpu.HBM((seq_size, block), jnp.int32), jax.ShapeDtypeStruct((taps * block, chunk), bf16))
        + (bundle,) * 4
        + (jax.ShapeDtypeStruct((2, channels, taps * channels), bf16),),
        in_specs=[
            scalars(),
            copied((1, block)),
            copied(phoneme_rows.shape),
            copied(conv_first.shape),
            copied(conv_second.shape),
        ],
        out_specs=(anywhere,) + (whole(),) * 6,
        scratch_shapes=[VMEM((seq_size, block), jnp.int32), pltpu.SemaphoreType.DMA],
    )(where, in_hbm(dur), in_hbm(phoneme_rows), in_hbm(conv_first), in_hbm(conv_second))
    bundles, turned = made[:4], made[4]

    *bundles, left, right = call(
        pieces_kernel,
        "pieces",
        vmem=8,
        flops=2 * 2 * EDGE * width * taps * chunk,
        moved=2 * taps * width * chunk,
        out_shape=(bundle,) * 4 + (pack,) * 2,
        in_specs=[scalars()] + [whole()] * 8,
        out_specs=(whole(),) * 6,
        input_output_aliases={5 + d: d for d in range(4)},
        scratch_shapes=[VMEM((2 * EDGE, width), f32), VMEM((taps, block + 2 * EDGE, chunk), bf16)],
    )(where, products, from_mate, from_outer, far, *bundles)

    order = (1, 3, 2)
    everyone = lax.all_to_all(spread, "seq", 0, 0, tiled=True)
    opposite = rotate(bundles[2], "mp", 2)
    bundles = [bundles[0], rotate(bundles[1], "mp", 1), rotate(bundles[3], "mp", 3), opposite]

    per_tile = 2 * channels * TILE
    thin = jax.ShapeDtypeStruct((most, 2, TILE), f32)
    slot = jax.ShapeDtypeStruct((2, frames), f32)
    reach = (2 * REACH + 1) * frames + 2 * TILE + 256
    near_shape = (NEAR, 2, 3, channels, TILE)
    far_shape = (most - NEAR, 2, 3, channels, TILE)
    ordered = [bundles[i] for i in (0, 1, 3, 2)]
    pred, offset, near, kept = call(
        functools.partial(forward_kernel, last_seq),
        "forward",
        flops=2 * per_tile * 2 * (taps * window + taps * channels),
        moved=2 * per_tile * 6,
        out_shape=(
            thin,
            jax.ShapeDtypeStruct((2,), jnp.int32),
            jax.ShapeDtypeStruct(near_shape, bf16),
            pltpu.HBM(far_shape, bf16),
        ),
        in_specs=[scalars()] + [whole()] * 8,
        out_specs=(whole(), scalars(), whole(), anywhere),
        scratch_shapes=[
            VMEM((2, window, TILE), f32),
            VMEM((2 * channels, taps * window), bf16),
            VMEM((2, channels, TILE), f32),
            VMEM(far_shape, bf16),
            pltpu.SemaphoreType.DMA((most - NEAR,)),
        ],
    )(where, to_mate, left, right, *ordered, turned)

    residual, kept, *slots = call(
        align_kernel,
        "align",
        vmem=4,
        moved=most * 8 * TILE * 8,
        out_shape=(thin, jax.ShapeDtypeStruct(far_shape, bf16)) + (slot,) * 5,
        in_specs=[scalars(), scalars()] + [whole()] * 7 + [anywhere],
        out_specs=(whole(),) * 7,
        scratch_shapes=[
            VMEM((8, reach), f32),
            VMEM((8, reach), f32),
            pltpu.SemaphoreType.DMA((most - NEAR,)),
        ],
    )(where, offset, everyone, pred, to_mate, left, right, far, bundles[1], in_hbm(kept))

    arrived = [
        lax.ppermute(slots[3], "seq", [(s, s ^ 1) for s in range(seq_size)]),
        lax.ppermute(slots[1], "seq", [(s, outer_of(s)) for s in range(seq_size)]),
        rotate(slots[4], "seq", REACH),
        rotate(slots[0], "seq", -REACH),
    ]

    sums = call(
        functools.partial(backward_kernel, last_seq),
        "backward",
        flops=2 * per_tile * 2 * (taps * share + taps * channels),
        moved=2 * per_tile * 6,
        out_shape=jax.ShapeDtypeStruct((taps * share, 2 * channels), bf16),
        in_specs=[scalars()] + [whole()] * 7,
        out_specs=whole(),
        scratch_shapes=[
            VMEM((2, share, TILE), f32),
            VMEM((taps * share, 2 * channels), f32),
            VMEM(conv_second.shape, bf16),
        ],
    )(where, to_mate, left, right, residual, near, kept, turned)

    merged = call(
        merge_kernel,
        "merge",
        vmem=4,
        moved=taps * share * channels * 8,
        out_shape=jax.ShapeDtypeStruct((taps * share + 16, frames // 2), bf16),
        in_specs=[whole()] * 6,
        out_specs=whole(),
    )(sums, slots[REACH], *arrived)

    mergeds = [merged, *(rotate(merged, "mp", d) for d in order)]
    predicted, row_grad = call(
        finish_kernel,
        "finish",
        vmem=8,
        flops=2 * block * features * taps * 2 * channels,
        moved=8 * taps * features * chunk,
        out_shape=(slot, jax.ShapeDtypeStruct((block, features), bf16)),
        in_specs=[scalars()] + [whole()] * 8,
        out_specs=(copied((2, frames)), copied((block, features))),
        scratch_shapes=[VMEM((taps, block, 2 * channels), bf16)],
    )(where, *(mergeds[i] for i in (0, 1, 3, 2)), *ordered)
    return (predicted, row_grad)


def solution(mesh):
    in_specs = (P("seq", None), P("seq"), P(None, None, "mp"), P(), P(), P(None, "seq"))
    out_specs = (P(None, "seq"), P("seq", "mp"))
    return jax.shard_map(body, mesh=mesh, in_specs=in_specs, out_specs=out_specs, check_vma=False)
```

profile of v0, /device:TPU:0, one launch (start us, length us, event | category | flops | bytes accessed | tf_op | source)
XLA Modules:
  0.0 57.4 jit_solution(11910159797036318804)
XLA Ops:
  0.6 0.1 pad_add_fusion.where_ref
  0.7 0.8 %pack.1 = (f32[8,1024]{1,0:T(8,128)S(1)}, f32[8,1024]{1,0:T(8,128)S(1)}) custom-call(s32[2]{0:T(128)S(1)} %pad_add_fusion.where_ref, s32[1,128]{1,0:T(1,128)} %bitcast.9, f32[2,1024]{1,0:T(2,128)} %targets_ref.1, bf16[2,256]{1,0:T(2,128)(2,1)} %readout_ref.1, bf16[128,1024]{1,0:T(8,128)(2,1)} %rows_ref.1, bf16[128,1024]{1,0:T(8,128)(2,1)} %rows_ref.1), custom_call_target="tpu_custom_call" | custom-call | bytes 65536 | tf_op jit(solution)/shard_map/pack/pallas_call | solution.py:501
  1.6 6.1 %collective-permute-start.1 = (f32[8,1024]{1,0:T(8,128)S(1)}, f32[8,1024]{1,0:T(8,128)S(1)}, u32[]{:S(2)}, u32[]{:S(2)}) collective-permute-start(f32[8,1024]{1,0:T(8,128)S(1)} %get-tuple-element.30), channel_id=1, source_target_pairs={{0,252},{4,8},{8,4},{12,16},{16,12},{20,24},{24,20},{28,32},{32,28... | collective-permute-start | bytes 98312 | tf_op jit(solution)/shard_map/ppermute | solution.py:522
  7.7 0.0 collective-permute-start
  7.7 0.0 collective-permute-start.2
  7.7 2.4 %prepare.1 = (s32[64,128]{1,0:T(8,128)}, bf16[384,128]{1,0:T(8,128)(2,1)S(1)}, bf16[1008,128]{1,0:T(8,128)(2,1)S(1)}, bf16[1008,128]{1,0:T(8,128)(2,1)S(1)}, bf1...) custom-call(s32[2]{0:T(128)S(1)} %pad_add_fusion.where_ref, ...), custom_call_target="tpu_custom_call" | custom-call | flops 100663296 | bytes 1835008 | tf_op jit(solution)/shard_map/prepare/pallas_call | solution.py:534
  10.1 4.8 %collective-permute-done.2.far_ref = f32[2,1024]{1,0:T(2,128)S(1)} collective-permute-done((f32[2,1024]{1,0:T(2,128)}, f32[2,1024]{1,0:T(2,128)S(1)}, u32[]{:S(2)}, u32[]{:S(2)}) %collective-permute-start.2) | collective-permute-done | bytes 8224 | tf_op jit(solution)/shard_map/ppermute | solution.py:523
  14.8 0.0 collective-permute-done.1.outer_ref
  14.9 0.0 collective-permute-done.mate_ref
  14.9 0.8 %pieces.1 = (bf16[1008,128]{1,0:T(8,128)(2,1)S(1)}, bf16[1008,128]{1,0:T(8,128)(2,1)S(1)}, bf16[1008,128]{1,0:T(8,128)(2,1)S(1)}, bf16[1008,128]{1,0:T(8,128)(2,...) custom-call(s32[2]{0:T(128)S(1)} %pad_add_fusion.where_ref, ...), custom_call_target="tpu_custom_call", output_to_operand_aliasing={{0}: (5, {}), {1}: (6, {}), {2}: (7, {}), {3}: (8, {})} | custom-call | flops 25165824 | bytes 786432 | tf_op jit(solution)/shard_map/pieces/pallas_call | solution.py:555
  15.7 0.1 collective-permute-start.3
  15.7 3.1 %collective-permute-start.4 = (bf16[1008,128]{1,0:T(8,128)(2,1)S(1)}, bf16[1008,128]{1,0:T(8,128)(2,1)S(1)}, u32[]{:S(2)}, u32[]{:S(2)}) collective-permute-start(bf16[1008,128]{1,0:T(8,128)(2,1)S(1)} %get-tuple-element.39), channel_id=1, source_target_pairs={{0,2},{1,3},{2,0},{3,1},{4,6},{5,7},{6,4},{7,5},{8,10},{9,11},{10,... | collective-permute-start | bytes 774152 | tf_op jit(solution)/shard_map/ppermute | solution.py:54
  18.9 2.5 %collective-permute-start.5 = (bf16[1008,128]{1,0:T(8,128)(2,1)S(1)}, bf16[1008,128]{1,0:T(8,128)(2,1)S(1)}, u32[]{:S(2)}, u32[]{:S(2)}) collective-permute-start(bf16[1008,128]{1,0:T(8,128)(2,1)S(1)} %get-tuple-element.40), channel_id=1, source_target_pairs={{0,3},{1,0},{2,1},{3,2},{4,7},{5,4},{6,5},{7,6},{8,11},{9,8},{10,9... | collective-permute-start | bytes 774152 | tf_op jit(solution)/shard_map/ppermute | solution.py:54
  21.4 4.6 %all-to-all-start = ((s32[64,1,128]{2,1,0:T(1,128)}), s32[64,1,128]{2,1,0:T(1,128)S(1)}, u32[]{:S(2)}, u32[]{:S(2)}) async-start(s32[64,1,128]{2,1,0:T(1,128)} %bitcast.8), calls=%async_computation | async-start | bytes 65536 | tf_op jit(solution)/shard_map/all_to_all | solution.py:569
  26.0 4.0 %collective-permute-done.4.two_ref.refs_6_ = bf16[1008,128]{1,0:T(8,128)(2,1)S(1)} collective-permute-done((bf16[1008,128]{1,0:T(8,128)(2,1)S(1)}, bf16[1008,128]{1,0:T(8,128)(2,1)S(1)}, u32[]{:S(2)}, u32[]{:S(2)}) %collective-permute-start.4) | collective-permute-done | bytes 258080 | tf_op jit(solution)/shard_map/ppermute | solution.py:54
  30.0 0.5 collective-permute-done.5.three_ref.refs_7_
  30.6 4.7 %forward.1 = (f32[3,2,512]{2,1,0:T(2,128)S(1)}, s32[2]{0:T(128)S(1)}, bf16[1,2,3,256,512]{4,3,2,1,0:T(8,128)(2,1)S(1)}, bf16[2,2,3,256,512]{4,3,2,1,0:T(8,128)(2,1)}) custom-call(s32[2]{0:T(128)S(1)} %pad_add_fusion.where_ref, f32[8,1024]{1,0:T(8,128)S(1)} %get-tuple-element.28.own_ref, f32[8,1024]{1,0:T(8,128)S(1)} %get-tuple-element.35.left_ref, ...), custom_call_target="tpu_custom_call" | custom-call | flops 1006632960 | bytes 3145728 | tf_op jit(solution)/shard_map/forward/pallas_call | solution.py:580
  35.3 0.1 all-to-all-done
  35.4 0.8 %align.1 = (f32[3,2,512]{2,1,0:T(2,128)S(1)}, bf16[2,2,3,256,512]{4,3,2,1,0:T(8,128)(2,1)S(1)}, f32[2,1024]{1,0:T(2,128)S(1)}, f32[2,1024]{1,0:T(2,128)S(1)}, f3...) custom-call(s32[2]{0:T(128)S(1)} %pad_add_fusion.where_ref, s32[2]{0:T(128)S(1)} %get-tuple-element.42.offset_ref, ...), custom_call_target="tpu_custom_call" | custom-call | bytes 98304 | tf_op jit(solution)/shard_map/align/pallas_call | solution.py:602
  36.2 0.3 collective-permute-start.6
  36.5 1.5 %collective-permute-start.7 = (f32[2,1024]{1,0:T(2,128)S(1)}, f32[2,1024]{1,0:T(2,128)S(1)}, u32[]{:S(2)}, u32[]{:S(2)}) collective-permute-start(f32[2,1024]{1,0:T(2,128)S(1)} %get-tuple-element.51), channel_id=1, source_target_pairs={{0,252},{4,8},{8,4},{12,16},{16,12},{20,24},{24,20},{28,32},{32,28... | collective-permute-start | bytes 24584 | tf_op jit(solution)/shard_map/ppermute | solution.py:619
  38.0 0.7 %collective-permute-start.8 = (f32[2,1024]{1,0:T(2,128)S(1)}, f32[2,1024]{1,0:T(2,128)S(1)}, u32[]{:S(2)}, u32[]{:S(2)}) collective-permute-start(f32[2,1024]{1,0:T(2,128)S(1)} %get-tuple-element.52), channel_id=1, source_target_pairs={{0,8},{4,12},{8,16},{12,20},{16,24},{20,28},{24,32},{28,36},{32,40... | collective-permute-start | bytes 24584 | tf_op jit(solution)/shard_map/ppermute | solution.py:54
  38.6 4.7 %collective-permute-start.9 = (f32[2,1024]{1,0:T(2,128)S(1)}, f32[2,1024]{1,0:T(2,128)S(1)}, u32[]{:S(2)}, u32[]{:S(2)}) collective-permute-start(f32[2,1024]{1,0:T(2,128)S(1)} %get-tuple-element.53), channel_id=1, source_target_pairs={{0,248},{4,252},{8,0},{12,4},{16,8},{20,12},{24,16},{28,20},{32,24... | collective-permute-start | bytes 24584 | tf_op jit(solution)/shard_map/ppermute | solution.py:54
  43.3 2.2 %backward.1.sums_ref = bf16[96,512]{1,0:T(8,128)(2,1)S(1)} custom-call(s32[2]{0:T(128)S(1)} %pad_add_fusion.where_ref, f32[8,1024]{1,0:T(8,128)S(1)} %get-tuple-element.28.own_ref, f32[8,1024]{1,0:T(8,128)S(1)} %get-tuple-element.35.left_ref, f32[8,1024]{1,0:T(8,128)S(1)} %get-tuple-element.36.right_ref, f32[3,2,512]{2,1,0:T(2,128)S(1)} %get-tuple-element.46.residual_ref, ...), custom_call_target="tpu_custom_call" | custom-call | flops 905969664 | bytes 3145728 | tf_op jit(solution)/shard_map/backward/pallas_call | solution.py:624
  45.5 0.0 collective-permute-done.6.refs_0_
  45.6 2.7 %collective-permute-start.12 = (bf16[112,512]{1,0:T(8,128)(2,1)S(1)}, bf16[112,512]{1,0:T(8,128)(2,1)S(1)}, u32[]{:S(2)}, u32[]{:S(2)}) collective-permute-start(bf16[112,512]{1,0:T(8,128)(2,1)S(1)} %merge.1.refs_0_), channel_id=1, source_target_pairs={{0,3},{1,0},{2,1},{3,2},{4,7},{5,4},{6,5},{7,6},{8,11},{9,8},{10,9... | collective-permute-start | bytes 344072 | tf_op jit(solution)/shard_map/ppermute | solution.py:54
  48.3 1.1 %collective-permute-start.11 = (bf16[112,512]{1,0:T(8,128)(2,1)S(1)}, bf16[112,512]{1,0:T(8,128)(2,1)S(1)}, u32[]{:S(2)}, u32[]{:S(2)}) collective-permute-start(bf16[112,512]{1,0:T(8,128)(2,1)S(1)} %merge.1.refs_0_), channel_id=1, source_target_pairs={{0,2},{1,3},{2,0},{3,1},{4,6},{5,7},{6,4},{7,5},{8,10},{9,11},{10,... | collective-permute-start | bytes 344072 | tf_op jit(solution)/shard_map/ppermute | solution.py:54
  49.4 0.7 %collective-permute-start.10 = (bf16[112,512]{1,0:T(8,128)(2,1)S(1)}, bf16[112,512]{1,0:T(8,128)(2,1)S(1)}, u32[]{:S(2)}, u32[]{:S(2)}) collective-permute-start(bf16[112,512]{1,0:T(8,128)(2,1)S(1)} %merge.1.refs_0_), channel_id=1, source_target_pairs={{0,1},{1,2},{2,3},{3,0},{4,5},{5,6},{6,7},{7,4},{8,9},{9,10},{10,1... | collective-permute-start | bytes 344072 | tf_op jit(solution)/shard_map/ppermute | solution.py:54
  50.1 2.0 %collective-permute-done.12.refs_3_ = bf16[112,512]{1,0:T(8,128)(2,1)S(1)} collective-permute-done((bf16[112,512]{1,0:T(8,128)(2,1)S(1)}, bf16[112,512]{1,0:T(8,128)(2,1)S(1)}, u32[]{:S(2)}, u32[]{:S(2)}) %collective-permute-start.12) | collective-permute-done | bytes 114720 | tf_op jit(solution)/shard_map/ppermute | solution.py:54
  52.1 2.5 %collective-permute-done.11.refs_2_ = bf16[112,512]{1,0:T(8,128)(2,1)S(1)} collective-permute-done((bf16[112,512]{1,0:T(8,128)(2,1)S(1)}, bf16[112,512]{1,0:T(8,128)(2,1)S(1)}, u32[]{:S(2)}, u32[]{:S(2)}) %collective-permute-start.11) | collective-permute-done | bytes 114720 | tf_op jit(solution)/shard_map/ppermute | solution.py:54
  54.6 1.2 %collective-permute-done.10.refs_1_ = bf16[112,512]{1,0:T(8,128)(2,1)S(1)} collective-permute-done((bf16[112,512]{1,0:T(8,128)(2,1)S(1)}, bf16[112,512]{1,0:T(8,128)(2,1)S(1)}, u32[]{:S(2)}, u32[]{:S(2)}) %collective-permute-start.10) | collective-permute-done | bytes 114720 | tf_op jit(solution)/shard_map/ppermute | solution.py:54
  55.8 1.6 %finish.1 = (f32[2,1024]{1,0:T(2,128)}, bf16[128,256]{1,0:T(8,128)(2,1)}) custom-call(s32[2]{0:T(128)S(1)} %pad_add_fusion.where_ref, bf16[112,512]{1,0:T(8,128)(2,1)S(1)} %merge.1.refs_0_, bf16[112,512]{1,0:T(8,128)(2,1)S(1)} %collective-permute-done.10.refs_1_, bf16[112,512]{1,0:T(8,128)(2,1)S(1)} %collective-permute-done.11.refs_2_, ...), custom_call_target="tpu_custom_call" | custom-call | flops 100663296 | bytes 786432 | tf_op jit(solution)/shard_map/finish/pallas_call | solution.py:650
  (5 shorter events, 0.1 us)
Async XLA Ops:
  1.6 13.3 %collective-permute-start.1 = (f32[8,1024]{1,0:T(8,128)S(1)}, f32[8,1024]{1,0:T(8,128)S(1)}, u32[]{:S(2)}, u32[]{:S(2)}) collective-permute-start(f32[8,1024]{1,0:T(8,128)S(1)} %get-tuple-element.30), channel_id=1, source_target_pairs={{0,252},{4,8},{8,4},{12,16},{16,12},{20,24},{24,20},{28,32},{32,28... | collective-permute-start | bytes 98312 | tf_op jit(solution)/shard_map/ppermute | solution.py:522
  7.7 7.2 %collective-permute-start = (f32[8,1024]{1,0:T(8,128)S(1)}, f32[8,1024]{1,0:T(8,128)S(1)}, u32[]{:S(2)}, u32[]{:S(2)}) collective-permute-start(f32[8,1024]{1,0:T(8,128)S(1)} %get-tuple-element.28.own_ref), channel_id=1, source_target_pairs={{0,4},{4,0},{8,12},{12,8},{16,20},{20,16},{24,28},{28,24},{32,36},... | collective-permute-start | bytes 98312 | tf_op jit(solution)/shard_map/ppermute | solution.py:521
  7.7 7.2 %collective-permute-start.2 = (f32[2,1024]{1,0:T(2,128)}, f32[2,1024]{1,0:T(2,128)S(1)}, u32[]{:S(2)}, u32[]{:S(2)}) collective-permute-start(f32[2,1024]{1,0:T(2,128)} %targets_ref.1), channel_id=1, source_target_pairs={{248,0},{9,1},{250,2},{11,3},{252,4},{13,5},{254,6},{15,7},{0,8},{... | collective-permute-start | bytes 24584 | tf_op jit(solution)/shard_map/ppermute | solution.py:523
  15.7 10.3 %collective-permute-start.3 = (bf16[1008,128]{1,0:T(8,128)(2,1)S(1)}, bf16[1008,128]{1,0:T(8,128)(2,1)S(1)}, u32[]{:S(2)}, u32[]{:S(2)}) collective-permute-start(bf16[1008,128]{1,0:T(8,128)(2,1)S(1)} %get-tuple-element.38), channel_id=1, source_target_pairs={{0,1},{1,2},{2,3},{3,0},{4,5},{5,6},{6,7},{7,4},{8,9},{9,10},{10,1... | collective-permute-start | bytes 774152 | tf_op jit(solution)/shard_map/ppermute | solution.py:54
  15.7 14.3 %collective-permute-start.4 = (bf16[1008,128]{1,0:T(8,128)(2,1)S(1)}, bf16[1008,128]{1,0:T(8,128)(2,1)S(1)}, u32[]{:S(2)}, u32[]{:S(2)}) collective-permute-start(bf16[1008,128]{1,0:T(8,128)(2,1)S(1)} %get-tuple-element.39), channel_id=1, source_target_pairs={{0,2},{1,3},{2,0},{3,1},{4,6},{5,7},{6,4},{7,5},{8,10},{9,11},{10,... | collective-permute-start | bytes 774152 | tf_op jit(solution)/shard_map/ppermute | solution.py:54
  18.9 11.7 %collective-permute-start.5 = (bf16[1008,128]{1,0:T(8,128)(2,1)S(1)}, bf16[1008,128]{1,0:T(8,128)(2,1)S(1)}, u32[]{:S(2)}, u32[]{:S(2)}) collective-permute-start(bf16[1008,128]{1,0:T(8,128)(2,1)S(1)} %get-tuple-element.40), channel_id=1, source_target_pairs={{0,3},{1,0},{2,1},{3,2},{4,7},{5,4},{6,5},{7,6},{8,11},{9,8},{10,9... | collective-permute-start | bytes 774152 | tf_op jit(solution)/shard_map/ppermute | solution.py:54
  21.4 14.0 %all-to-all-start = ((s32[64,1,128]{2,1,0:T(1,128)}), s32[64,1,128]{2,1,0:T(1,128)S(1)}, u32[]{:S(2)}, u32[]{:S(2)}) async-start(s32[64,1,128]{2,1,0:T(1,128)} %bitcast.8), calls=%async_computation | async-start | bytes 65536 | tf_op jit(solution)/shard_map/all_to_all | solution.py:569
  36.2 9.3 %collective-permute-start.6 = (f32[2,1024]{1,0:T(2,128)S(1)}, f32[2,1024]{1,0:T(2,128)S(1)}, u32[]{:S(2)}, u32[]{:S(2)}) collective-permute-start(f32[2,1024]{1,0:T(2,128)S(1)} %get-tuple-element.50), channel_id=1, source_target_pairs={{0,4},{4,0},{8,12},{12,8},{16,20},{20,16},{24,28},{28,24},{32,36},... | collective-permute-start | bytes 24584 | tf_op jit(solution)/shard_map/ppermute | solution.py:618
  36.5 9.0 %collective-permute-start.7 = (f32[2,1024]{1,0:T(2,128)S(1)}, f32[2,1024]{1,0:T(2,128)S(1)}, u32[]{:S(2)}, u32[]{:S(2)}) collective-permute-start(f32[2,1024]{1,0:T(2,128)S(1)} %get-tuple-element.51), channel_id=1, source_target_pairs={{0,252},{4,8},{8,4},{12,16},{16,12},{20,24},{24,20},{28,32},{32,28... | collective-permute-start | bytes 24584 | tf_op jit(solution)/shard_map/ppermute | solution.py:619
  38.0 7.5 %collective-permute-start.8 = (f32[2,1024]{1,0:T(2,128)S(1)}, f32[2,1024]{1,0:T(2,128)S(1)}, u32[]{:S(2)}, u32[]{:S(2)}) collective-permute-start(f32[2,1024]{1,0:T(2,128)S(1)} %get-tuple-element.52), channel_id=1, source_target_pairs={{0,8},{4,12},{8,16},{12,20},{16,24},{20,28},{24,32},{28,36},{32,40... | collective-permute-start | bytes 24584 | tf_op jit(solution)/shard_map/ppermute | solution.py:54
  38.6 6.9 %collective-permute-start.9 = (f32[2,1024]{1,0:T(2,128)S(1)}, f32[2,1024]{1,0:T(2,128)S(1)}, u32[]{:S(2)}, u32[]{:S(2)}) collective-permute-start(f32[2,1024]{1,0:T(2,128)S(1)} %get-tuple-element.53), channel_id=1, source_target_pairs={{0,248},{4,252},{8,0},{12,4},{16,8},{20,12},{24,16},{28,20},{32,24... | collective-permute-start | bytes 24584 | tf_op jit(solution)/shard_map/ppermute | solution.py:54
  45.6 6.5 %collective-permute-start.12 = (bf16[112,512]{1,0:T(8,128)(2,1)S(1)}, bf16[112,512]{1,0:T(8,128)(2,1)S(1)}, u32[]{:S(2)}, u32[]{:S(2)}) collective-permute-start(bf16[112,512]{1,0:T(8,128)(2,1)S(1)} %merge.1.refs_0_), channel_id=1, source_target_pairs={{0,3},{1,0},{2,1},{3,2},{4,7},{5,4},{6,5},{7,6},{8,11},{9,8},{10,9... | collective-permute-start | bytes 344072 | tf_op jit(solution)/shard_map/ppermute | solution.py:54
  48.3 6.3 %collective-permute-start.11 = (bf16[112,512]{1,0:T(8,128)(2,1)S(1)}, bf16[112,512]{1,0:T(8,128)(2,1)S(1)}, u32[]{:S(2)}, u32[]{:S(2)}) collective-permute-start(bf16[112,512]{1,0:T(8,128)(2,1)S(1)} %merge.1.refs_0_), channel_id=1, source_target_pairs={{0,2},{1,3},{2,0},{3,1},{4,6},{5,7},{6,4},{7,5},{8,10},{9,11},{10,... | collective-permute-start | bytes 344072 | tf_op jit(solution)/shard_map/ppermute | solution.py:54
  49.4 6.4 %collective-permute-start.10 = (bf16[112,512]{1,0:T(8,128)(2,1)S(1)}, bf16[112,512]{1,0:T(8,128)(2,1)S(1)}, u32[]{:S(2)}, u32[]{:S(2)}) collective-permute-start(bf16[112,512]{1,0:T(8,128)(2,1)S(1)} %merge.1.refs_0_), channel_id=1, source_target_pairs={{0,1},{1,2},{2,3},{3,0},{4,5},{5,6},{6,7},{7,4},{8,9},{9,10},{10,1... | collective-permute-start | bytes 344072 | tf_op jit(solution)/shard_map/ppermute | solution.py:54
where the time goes:
time: 57.6 us; the launch traced here: 57.4 us
  starting transfers between devices  28 us (49%)
  waiting for transfers between devices  15.2 us (26%)
  Pallas kernels  13.3 us (23%)
  between operations  0.76 us (1%)
    ppermute x8, starting transfers between devices, rotate(): lax.ppermute(block, axis, [(i, (i + distance) % size) for i in range(size)])  15.6 us
    ppermute x8, waiting for transfers between devices, rotate(): lax.ppermute(block, axis, [(i, (i + distance) % size) for i in range(size)])  10.3 us
    ppermute x1, starting transfers between devices, body(): lax.ppermute(to_outer, 'seq', [(s, outer_of(s)) for s in range(seq_size)])  6.1 us
    ppermute x1, waiting for transfers between devices, body(): lax.ppermute(targets, ('seq', 'mp'), [((s + (-REACH if m % 2 == 0 else RE...  4.78 us
    pallas_call x1, Pallas kernels, body(): call(functools.partial(forward_kernel, last_seq), 'forward', flops=2 * pe...  4.7 us
    all_to_all x1, starting transfers between devices, body(): everyone = lax.all_to_all(spread, 'seq', 0, 0, tiled=True)  4.59 us
    pallas_call x1, Pallas kernels, body(): call(prepare_kernel, 'prepare', vmem=12, flops=2 * block * width * taps *...  2.39 us
    pallas_call x1, Pallas kernels, body(): call(functools.partial(backward_kernel, last_seq), 'backward', flops=2 *...  2.16 us
  transfers between devices with their start and end apart: 14, of which 7 were waited for; matrix products, arithmetic and copies ran while one was open for 0% of the time, Pallas kernels for 16%

commit v1 on v0

--- a/solution.py
+++ b/solution.py
@@ -258,28 +258,32 @@
         )
         inside = jnp.where((frames >= lowest) & (frames < end), 1.0, 0.0)
         answered = jnp.where((lane >= 2) & (lane < 2 + STRIDE), inside, 0.0)
-        for q in range(2):
-            low, high = q * channels, (q + 1) * channels
-            first = jnp.dot(table_ref[low:high, :], selector, preferred_element_type=f32)
-            act = (jnp.maximum(first, 0.0) + jnp.log(1.0 + jnp.exp(-jnp.abs(first)))).astype(bf16).astype(f32)
-            centered = act - column_mean(act)
-            inverse_one = lax.rsqrt(column_mean(centered * centered) + EPSILON)
-            hidden = centered * (inverse_one * inside)
-            kept_ref[at, q, 2] = ((1.0 - jnp.exp(-act)) * (inverse_one * answered)).astype(bf16)
-            stacked = with_neighbours(hidden)
-            kept_ref[at, q, 0] = stacked[channels : 2 * channels]
-            second = jnp.dot(kernel_ref[q], stacked, preferred_element_type=f32)
-            small = jnp.exp(-jnp.abs(second))
-            soft = jnp.maximum(second, 0.0) + jnp.log(1.0 + small)
-            sigmoid = jnp.exp(second - soft)
-            centered = soft - column_mean(soft)
-            inverse_two = lax.rsqrt(column_mean(centered * centered) + EPSILON)
-            normed = centered * inverse_two
+        both = range(2)
+        first = [
+            jnp.dot(table_ref[q * channels : (q + 1) * channels, :], selector, preferred_element_type=f32)
+            for q in both
+        ]
+        act = [
+            (jnp.maximum(x, 0.0) + jnp.log(1.0 + jnp.exp(-jnp.abs(x)))).astype(bf16).astype(f32) for x in first
+        ]
+        centered = [x - column_mean(x) for x in act]
+        inverse_one = [lax.rsqrt(column_mean(x * x) + EPSILON) for x in centered]
+        stacked = [with_neighbours(centered[q] * (inverse_one[q] * inside)) for q in both]
+        second = [jnp.dot(kernel_ref[q], stacked[q], preferred_element_type=f32) for q in both]
+        for q in both:
+            kept_ref[at, q, 2] = ((1.0 - jnp.exp(-act[q])) * (inverse_one[q] * answered)).astype(bf16)
+            kept_ref[at, q, 0] = stacked[q][channels : 2 * channels]
+        soft = [jnp.maximum(x, 0.0) + jnp.log(1.0 + jnp.exp(-jnp.abs(x))) for x in second]
+        sigmoid = [jnp.exp(second[q] - soft[q]) for q in both]
+        centered = [x - column_mean(x) for x in soft]
+        inverse_two = [lax.rsqrt(column_mean(x * x) + EPSILON) for x in centered]
+        normed = [centered[q] * inverse_two[q] for q in both]
+        weighted_mean = [column_mean(normed[q] * weight_ref[q]) for q in both]
+        for q in both:
             weights = weight_ref[q]
-            weighted_mean = column_mean(normed * weights)
-            pred_ref[t, q : q + 1, :] = weighted_mean * float(channels)
-            factor = (weights - column_mean(weights) - normed * weighted_mean) * sigmoid
-            kept_ref[at, q, 1] = (factor * (inverse_two * inside)).astype(bf16)
+            pred_ref[t, q : q + 1, :] = weighted_mean[q] * float(channels)
+            factor = (weights - column_mean(weights) - normed[q] * weighted_mean[q]) * sigmoid[q]
+            kept_ref[at, q, 1] = (factor * (inverse_two[q] * inside)).astype(bf16)
 
     def step(t, carry):
         work(t, near_ref, t)
@@ -401,21 +405,23 @@
         selector = jnp.concatenate(
             [one_hot(frames + (k - 1.0), bounds_ref[0], bounds_ref[1]) for k in range(taps)], axis=0
         )
-        for q in range(2):
-            low, high = q * channels, (q + 1) * channels
-            grad_second = kept_ref[at, q, 1].astype(f32) * residual_ref[t, q : q + 1, :]
-            stacked = with_neighbours(grad_second)
-            grad_hidden = jnp.zeros((channels, TILE), f32)
-            for k in range(taps):
-                part = stacked[(taps - 1 - k) * channels : (taps - k) * channels]
-                grad_hidden = grad_hidden + jnp.dot(conv_ref[q, k], part, preferred_element_type=f32)
-            normed = kept_ref[at, q, 0].astype(f32)
-            first_mean = column_mean(grad_hidden)
-            second_mean = column_mean(grad_hidden * normed)
-            scale = kept_ref[at, q, 2].astype(f32)
-            grad_first = (grad_hidden - first_mean - normed * second_mean) * scale
-            sums_ref[:, low:high] += lax.dot_general(
-                selector, grad_first.astype(bf16), (((1,), (1,)), ((), ())), preferred_element_type=f32
+        both = range(2)
+        stacked = [with_neighbours(kept_ref[at, q, 1].astype(f32) * residual_ref[t, q : q + 1, :]) for q in both]
+        grad_hidden = [jnp.zeros((channels, TILE), f32) for q in both]
+        for k in range(taps):
+            for q in both:
+                part = stacked[q][(taps - 1 - k) * channels : (taps - k) * channels]
+                grad_hidden[q] = grad_hidden[q] + jnp.dot(conv_ref[q, k], part, preferred_element_type=f32)
+        normed = [kept_ref[at, q, 0].astype(f32) for q in both]
+        first_mean = [column_mean(x) for x in grad_hidden]
+        second_mean = [column_mean(grad_hidden[q] * normed[q]) for q in both]
+        grad_first = [
+            (grad_hidden[q] - first_mean[q] - normed[q] * second_mean[q]) * kept_ref[at, q, 2].astype(f32)
+            for q in both
+        ]
+        for q in both:
+            sums_ref[:, q * channels : (q + 1) * channels] += lax.dot_general(
+                selector, grad_first[q].astype(bf16), (((1,), (1,)), ((), ())), preferred_element_type=f32
             )
 
     def step(t, carry):

time: 57.6 us -> 56.9 us (0.988)
  starting transfers between devices: 28 us -> 27.4 us
  transfers between devices with their start and end apart: 14 -> 14, of which waited for: 7 -> 7; matrix products, arithmetic and copies ran while one was open for 0% -> 0% of each run, Pallas kernels for 16% -> 15%
where the time goes in v1:
time: 56.9 us; the launch traced here: 56.7 us
  starting transfers between devices  27.4 us (48%)
  waiting for transfers between devices  15.6 us (27%)
  Pallas kernels  12.8 us (22%)
  between operations  0.76 us (1%)
    ppermute x8, starting transfers between devices, rotate(): lax.ppermute(block, axis, [(i, (i + distance) % size) for i in range(size)])  15.4 us
    ppermute x8, waiting for transfers between devices, rotate(): lax.ppermute(block, axis, [(i, (i + distance) % size) for i in range(size)])  10.3 us
    ppermute x1, starting transfers between devices, body(): lax.ppermute(to_outer, 'seq', [(s, outer_of(s)) for s in range(seq_size)])  6.1 us
    ppermute x1, waiting for transfers between devices, body(): lax.ppermute(targets, ('seq', 'mp'), [((s + (-REACH if m % 2 == 0 else RE...  4.78 us
    all_to_all x1, starting transfers between devices, body(): everyone = lax.all_to_all(spread, 'seq', 0, 0, tiled=True)  4.59 us
    pallas_call x1, Pallas kernels, body(): call(functools.partial(forward_kernel, last_seq), 'forward', flops=2 * pe...  4.28 us
    pallas_call x1, Pallas kernels, body(): call(prepare_kernel, 'prepare', vmem=12, flops=2 * block * width * taps *...  2.39 us
    pallas_call x1, Pallas kernels, body(): call(functools.partial(backward_kernel, last_seq), 'backward', flops=2 *...  2.09 us
  transfers between devices with their start and end apart: 14, of which 7 were waited for; matrix products, arithmetic and copies ran while one was open for 0% of the time, Pallas kernels for 15%

profile of v1, /device:TPU:0, one launch (start us, length us, event | category | flops | bytes accessed | tf_op | source)
XLA Modules:
  0.0 56.7 jit_solution(9070699689403380572)
XLA Ops:
  0.6 0.1 pad_add_fusion.where_ref
  0.7 0.8 %pack.1 = (f32[8,1024]{1,0:T(8,128)S(1)}, f32[8,1024]{1,0:T(8,128)S(1)}) custom-call(s32[2]{0:T(128)S(1)} %pad_add_fusion.where_ref, s32[1,128]{1,0:T(1,128)} %bitcast.9, f32[2,1024]{1,0:T(2,128)} %targets_ref.1, bf16[2,256]{1,0:T(2,128)(2,1)} %readout_ref.1, bf16[128,1024]{1,0:T(8,128)(2,1)} %rows_ref.1, bf16[128,1024]{1,0:T(8,128)(2,1)} %rows_ref.1), custom_call_target="tpu_custom_call" | custom-call | bytes 65536 | tf_op jit(solution)/shard_map/pack/pallas_call | solution.py:507
  1.6 6.1 %collective-permute-start.1 = (f32[8,1024]{1,0:T(8,128)S(1)}, f32[8,1024]{1,0:T(8,128)S(1)}, u32[]{:S(2)}, u32[]{:S(2)}) collective-permute-start(f32[8,1024]{1,0:T(8,128)S(1)} %get-tuple-element.30), channel_id=1, source_target_pairs={{0,252},{4,8},{8,4},{12,16},{16,12},{20,24},{24,20},{28,32},{32,28... | collective-permute-start | bytes 98312 | tf_op jit(solution)/shard_map/ppermute | solution.py:528
  7.7 2.4 %prepare.1 = (s32[64,128]{1,0:T(8,128)}, bf16[384,128]{1,0:T(8,128)(2,1)S(1)}, bf16[1008,128]{1,0:T(8,128)(2,1)S(1)}, bf16[1008,128]{1,0:T(8,128)(2,1)S(1)}, bf1...) custom-call(s32[2]{0:T(128)S(1)} %pad_add_fusion.where_ref, ...), custom_call_target="tpu_custom_call" | custom-call | flops 100663296 | bytes 1835008 | tf_op jit(solution)/shard_map/prepare/pallas_call | solution.py:540
  10.1 4.8 %collective-permute-done.2.far_ref = f32[2,1024]{1,0:T(2,128)S(1)} collective-permute-done((f32[2,1024]{1,0:T(2,128)}, f32[2,1024]{1,0:T(2,128)S(1)}, u32[]{:S(2)}, u32[]{:S(2)}) %collective-permute-start.2) | collective-permute-done | bytes 8224 | tf_op jit(solution)/shard_map/ppermute | solution.py:529
  14.8 0.0 collective-permute-done.1.outer_ref
  14.9 0.8 %pieces.1 = (bf16[1008,128]{1,0:T(8,128)(2,1)S(1)}, bf16[1008,128]{1,0:T(8,128)(2,1)S(1)}, bf16[1008,128]{1,0:T(8,128)(2,1)S(1)}, bf16[1008,128]{1,0:T(8,128)(2,...) custom-call(s32[2]{0:T(128)S(1)} %pad_add_fusion.where_ref, ...), custom_call_target="tpu_custom_call", output_to_operand_aliasing={{0}: (5, {}), {1}: (6, {}), {2}: (7, {}), {3}: (8, {})} | custom-call | flops 25165824 | bytes 786432 | tf_op jit(solution)/shard_map/pieces/pallas_call | solution.py:561
  15.7 0.1 collective-permute-start.3
  15.7 3.1 %collective-permute-start.4 = (bf16[1008,128]{1,0:T(8,128)(2,1)S(1)}, bf16[1008,128]{1,0:T(8,128)(2,1)S(1)}, u32[]{:S(2)}, u32[]{:S(2)}) collective-permute-start(bf16[1008,128]{1,0:T(8,128)(2,1)S(1)} %get-tuple-element.39), channel_id=1, source_target_pairs={{0,2},{1,3},{2,0},{3,1},{4,6},{5,7},{6,4},{7,5},{8,10},{9,11},{10,... | collective-permute-start | bytes 774152 | tf_op jit(solution)/shard_map/ppermute | solution.py:54
  18.9 2.5 %collective-permute-start.5 = (bf16[1008,128]{1,0:T(8,128)(2,1)S(1)}, bf16[1008,128]{1,0:T(8,128)(2,1)S(1)}, u32[]{:S(2)}, u32[]{:S(2)}) collective-permute-start(bf16[1008,128]{1,0:T(8,128)(2,1)S(1)} %get-tuple-element.40), channel_id=1, source_target_pairs={{0,3},{1,0},{2,1},{3,2},{4,7},{5,4},{6,5},{7,6},{8,11},{9,8},{10,9... | collective-permute-start | bytes 774152 | tf_op jit(solution)/shard_map/ppermute | solution.py:54
  21.4 4.6 %all-to-all-start = ((s32[64,1,128]{2,1,0:T(1,128)}), s32[64,1,128]{2,1,0:T(1,128)S(1)}, u32[]{:S(2)}, u32[]{:S(2)}) async-start(s32[64,1,128]{2,1,0:T(1,128)} %bitcast.8), calls=%async_computation | async-start | bytes 65536 | tf_op jit(solution)/shard_map/all_to_all | solution.py:575
  26.0 0.0 collective-permute-done.3.one_ref.refs_5_
  26.0 4.0 %collective-permute-done.4.two_ref.refs_6_ = bf16[1008,128]{1,0:T(8,128)(2,1)S(1)} collective-permute-done((bf16[1008,128]{1,0:T(8,128)(2,1)S(1)}, bf16[1008,128]{1,0:T(8,128)(2,1)S(1)}, u32[]{:S(2)}, u32[]{:S(2)}) %collective-permute-start.4) | collective-permute-done | bytes 258080 | tf_op jit(solution)/shard_map/ppermute | solution.py:54
  30.0 0.5 collective-permute-done.5.three_ref.refs_7_
  30.6 4.3 %forward.1 = (f32[3,2,512]{2,1,0:T(2,128)S(1)}, s32[2]{0:T(128)S(1)}, bf16[1,2,3,256,512]{4,3,2,1,0:T(8,128)(2,1)S(1)}, bf16[2,2,3,256,512]{4,3,2,1,0:T(8,128)(2,1)}) custom-call(s32[2]{0:T(128)S(1)} %pad_add_fusion.where_ref, f32[8,1024]{1,0:T(8,128)S(1)} %get-tuple-element.28.own_ref, f32[8,1024]{1,0:T(8,128)S(1)} %get-tuple-element.35.left_ref, ...), custom_call_target="tpu_custom_call" | custom-call | flops 1006632960 | bytes 3145728 | tf_op jit(solution)/shard_map/forward/pallas_call | solution.py:586
  34.9 0.6 all-to-all-done
  35.4 0.8 %align.1 = (f32[3,2,512]{2,1,0:T(2,128)S(1)}, bf16[2,2,3,256,512]{4,3,2,1,0:T(8,128)(2,1)S(1)}, f32[2,1024]{1,0:T(2,128)S(1)}, f32[2,1024]{1,0:T(2,128)S(1)}, f3...) custom-call(s32[2]{0:T(128)S(1)} %pad_add_fusion.where_ref, s32[2]{0:T(128)S(1)} %get-tuple-element.42.offset_ref, ...), custom_call_target="tpu_custom_call" | custom-call | bytes 98304 | tf_op jit(solution)/shard_map/align/pallas_call | solution.py:608
  36.2 0.1 collective-permute-start.6
  36.3 1.2 %collective-permute-start.7 = (f32[2,1024]{1,0:T(2,128)S(1)}, f32[2,1024]{1,0:T(2,128)S(1)}, u32[]{:S(2)}, u32[]{:S(2)}) collective-permute-start(f32[2,1024]{1,0:T(2,128)S(1)} %get-tuple-element.51), channel_id=1, source_target_pairs={{0,252},{4,8},{8,4},{12,16},{16,12},{20,24},{24,20},{28,32},{32,28... | collective-permute-start | bytes 24584 | tf_op jit(solution)/shard_map/ppermute | solution.py:625
  37.6 0.9 %collective-permute-start.8 = (f32[2,1024]{1,0:T(2,128)S(1)}, f32[2,1024]{1,0:T(2,128)S(1)}, u32[]{:S(2)}, u32[]{:S(2)}) collective-permute-start(f32[2,1024]{1,0:T(2,128)S(1)} %get-tuple-element.52), channel_id=1, source_target_pairs={{0,8},{4,12},{8,16},{12,20},{16,24},{20,28},{24,32},{28,36},{32,40... | collective-permute-start | bytes 24584 | tf_op jit(solution)/shard_map/ppermute | solution.py:54
  38.5 4.4 %collective-permute-start.9 = (f32[2,1024]{1,0:T(2,128)S(1)}, f32[2,1024]{1,0:T(2,128)S(1)}, u32[]{:S(2)}, u32[]{:S(2)}) collective-permute-start(f32[2,1024]{1,0:T(2,128)S(1)} %get-tuple-element.53), channel_id=1, source_target_pairs={{0,248},{4,252},{8,0},{12,4},{16,8},{20,12},{24,16},{28,20},{32,24... | collective-permute-start | bytes 24584 | tf_op jit(solution)/shard_map/ppermute | solution.py:54
  42.9 2.1 %backward.1.sums_ref = bf16[96,512]{1,0:T(8,128)(2,1)S(1)} custom-call(s32[2]{0:T(128)S(1)} %pad_add_fusion.where_ref, f32[8,1024]{1,0:T(8,128)S(1)} %get-tuple-element.28.own_ref, f32[8,1024]{1,0:T(8,128)S(1)} %get-tuple-element.35.left_ref, f32[8,1024]{1,0:T(8,128)S(1)} %get-tuple-element.36.right_ref, f32[3,2,512]{2,1,0:T(2,128)S(1)} %get-tuple-element.46.residual_ref, ...), custom_call_target="tpu_custom_call" | custom-call | flops 905969664 | bytes 3145728 | tf_op jit(solution)/shard_map/backward/pallas_call | solution.py:630
  45.0 0.0 collective-permute-done.6.refs_0_
  45.0 0.0 collective-permute-done.7.refs_1_
  45.0 0.0 collective-permute-done.9.refs_3_
  45.1 2.5 %collective-permute-start.12 = (bf16[112,512]{1,0:T(8,128)(2,1)S(1)}, bf16[112,512]{1,0:T(8,128)(2,1)S(1)}, u32[]{:S(2)}, u32[]{:S(2)}) collective-permute-start(bf16[112,512]{1,0:T(8,128)(2,1)S(1)} %merge.1.refs_0_), channel_id=1, source_target_pairs={{0,3},{1,0},{2,1},{3,2},{4,7},{5,4},{6,5},{7,6},{8,11},{9,8},{10,9... | collective-permute-start | bytes 344072 | tf_op jit(solution)/shard_map/ppermute | solution.py:54
  47.6 1.1 %collective-permute-start.11 = (bf16[112,512]{1,0:T(8,128)(2,1)S(1)}, bf16[112,512]{1,0:T(8,128)(2,1)S(1)}, u32[]{:S(2)}, u32[]{:S(2)}) collective-permute-start(bf16[112,512]{1,0:T(8,128)(2,1)S(1)} %merge.1.refs_0_), channel_id=1, source_target_pairs={{0,2},{1,3},{2,0},{3,1},{4,6},{5,7},{6,4},{7,5},{8,10},{9,11},{10,... | collective-permute-start | bytes 344072 | tf_op jit(solution)/shard_map/ppermute | solution.py:54
  48.8 0.7 %collective-permute-start.10 = (bf16[112,512]{1,0:T(8,128)(2,1)S(1)}, bf16[112,512]{1,0:T(8,128)(2,1)S(1)}, u32[]{:S(2)}, u32[]{:S(2)}) collective-permute-start(bf16[112,512]{1,0:T(8,128)(2,1)S(1)} %merge.1.refs_0_), channel_id=1, source_target_pairs={{0,1},{1,2},{2,3},{3,0},{4,5},{5,6},{6,7},{7,4},{8,9},{9,10},{10,1... | collective-permute-start | bytes 344072 | tf_op jit(solution)/shard_map/ppermute | solution.py:54
  49.4 2.1 %collective-permute-done.12.refs_3_ = bf16[112,512]{1,0:T(8,128)(2,1)S(1)} collective-permute-done((bf16[112,512]{1,0:T(8,128)(2,1)S(1)}, bf16[112,512]{1,0:T(8,128)(2,1)S(1)}, u32[]{:S(2)}, u32[]{:S(2)}) %collective-permute-start.12) | collective-permute-done | bytes 114720 | tf_op jit(solution)/shard_map/ppermute | solution.py:54
  51.5 2.5 %collective-permute-done.11.refs_2_ = bf16[112,512]{1,0:T(8,128)(2,1)S(1)} collective-permute-done((bf16[112,512]{1,0:T(8,128)(2,1)S(1)}, bf16[112,512]{1,0:T(8,128)(2,1)S(1)}, u32[]{:S(2)}, u32[]{:S(2)}) %collective-permute-start.11) | collective-permute-done | bytes 114720 | tf_op jit(solution)/shard_map/ppermute | solution.py:54
  54.0 1.2 %collective-permute-done.10.refs_1_ = bf16[112,512]{1,0:T(8,128)(2,1)S(1)} collective-permute-done((bf16[112,512]{1,0:T(8,128)(2,1)S(1)}, bf16[112,512]{1,0:T(8,128)(2,1)S(1)}, u32[]{:S(2)}, u32[]{:S(2)}) %collective-permute-start.10) | collective-permute-done | bytes 114720 | tf_op jit(solution)/shard_map/ppermute | solution.py:54
  55.1 1.6 %finish.1 = (f32[2,1024]{1,0:T(2,128)}, bf16[128,256]{1,0:T(8,128)(2,1)}) custom-call(s32[2]{0:T(128)S(1)} %pad_add_fusion.where_ref, bf16[112,512]{1,0:T(8,128)(2,1)S(1)} %merge.1.refs_0_, bf16[112,512]{1,0:T(8,128)(2,1)S(1)} %collective-permute-done.10.refs_1_, bf16[112,512]{1,0:T(8,128)(2,1)S(1)} %collective-permute-done.11.refs_2_, ...), custom_call_target="tpu_custom_call" | custom-call | flops 100663296 | bytes 786432 | tf_op jit(solution)/shard_map/finish/pallas_call | solution.py:656
  (5 shorter events, 0.1 us)
Async XLA Ops:
  1.6 13.3 %collective-permute-start.1 = (f32[8,1024]{1,0:T(8,128)S(1)}, f32[8,1024]{1,0:T(8,128)S(1)}, u32[]{:S(2)}, u32[]{:S(2)}) collective-permute-start(f32[8,1024]{1,0:T(8,128)S(1)} %get-tuple-element.30), channel_id=1, source_target_pairs={{0,252},{4,8},{8,4},{12,16},{16,12},{20,24},{24,20},{28,32},{32,28... | collective-permute-start | bytes 98312 | tf_op jit(solution)/shard_map/ppermute | solution.py:528
  7.7 7.2 %collective-permute-start = (f32[8,1024]{1,0:T(8,128)S(1)}, f32[8,1024]{1,0:T(8,128)S(1)}, u32[]{:S(2)}, u32[]{:S(2)}) collective-permute-start(f32[8,1024]{1,0:T(8,128)S(1)} %get-tuple-element.28.own_ref), channel_id=1, source_target_pairs={{0,4},{4,0},{8,12},{12,8},{16,20},{20,16},{24,28},{28,24},{32,36},... | collective-permute-start | bytes 98312 | tf_op jit(solution)/shard_map/ppermute | solution.py:527
  7.7 7.2 %collective-permute-start.2 = (f32[2,1024]{1,0:T(2,128)}, f32[2,1024]{1,0:T(2,128)S(1)}, u32[]{:S(2)}, u32[]{:S(2)}) collective-permute-start(f32[2,1024]{1,0:T(2,128)} %targets_ref.1), channel_id=1, source_target_pairs={{248,0},{9,1},{250,2},{11,3},{252,4},{13,5},{254,6},{15,7},{0,8},{... | collective-permute-start | bytes 24584 | tf_op jit(solution)/shard_map/ppermute | solution.py:529
  15.7 10.3 %collective-permute-start.3 = (bf16[1008,128]{1,0:T(8,128)(2,1)S(1)}, bf16[1008,128]{1,0:T(8,128)(2,1)S(1)}, u32[]{:S(2)}, u32[]{:S(2)}) collective-permute-start(bf16[1008,128]{1,0:T(8,128)(2,1)S(1)} %get-tuple-element.38), channel_id=1, source_target_pairs={{0,1},{1,2},{2,3},{3,0},{4,5},{5,6},{6,7},{7,4},{8,9},{9,10},{10,1... | collective-permute-start | bytes 774152 | tf_op jit(solution)/shard_map/ppermute | solution.py:54
  15.7 14.3 %collective-permute-start.4 = (bf16[1008,128]{1,0:T(8,128)(2,1)S(1)}, bf16[1008,128]{1,0:T(8,128)(2,1)S(1)}, u32[]{:S(2)}, u32[]{:S(2)}) collective-permute-start(bf16[1008,128]{1,0:T(8,128)(2,1)S(1)} %get-tuple-element.39), channel_id=1, source_target_pairs={{0,2},{1,3},{2,0},{3,1},{4,6},{5,7},{6,4},{7,5},{8,10},{9,11},{10,... | collective-permute-start | bytes 774152 | tf_op jit(solution)/shard_map/ppermute | solution.py:54
  18.9 11.7 %collective-permute-start.5 = (bf16[1008,128]{1,0:T(8,128)(2,1)S(1)}, bf16[1008,128]{1,0:T(8,128)(2,1)S(1)}, u32[]{:S(2)}, u32[]{:S(2)}) collective-permute-start(bf16[1008,128]{1,0:T(8,128)(2,1)S(1)} %get-tuple-element.40), channel_id=1, source_target_pairs={{0,3},{1,0},{2,1},{3,2},{4,7},{5,4},{6,5},{7,6},{8,11},{9,8},{10,9... | collective-permute-start | bytes 774152 | tf_op jit(solution)/shard_map/ppermute | solution.py:54
  21.4 14.0 %all-to-all-start = ((s32[64,1,128]{2,1,0:T(1,128)}), s32[64,1,128]{2,1,0:T(1,128)S(1)}, u32[]{:S(2)}, u32[]{:S(2)}) async-start(s32[64,1,128]{2,1,0:T(1,128)} %bitcast.8), calls=%async_computation | async-start | bytes 65536 | tf_op jit(solution)/shard_map/all_to_all | solution.py:575
  36.2 8.8 %collective-permute-start.6 = (f32[2,1024]{1,0:T(2,128)S(1)}, f32[2,1024]{1,0:T(2,128)S(1)}, u32[]{:S(2)}, u32[]{:S(2)}) collective-permute-start(f32[2,1024]{1,0:T(2,128)S(1)} %get-tuple-element.50), channel_id=1, source_target_pairs={{0,4},{4,0},{8,12},{12,8},{16,20},{20,16},{24,28},{28,24},{32,36},... | collective-permute-start | bytes 24584 | tf_op jit(solution)/shard_map/ppermute | solution.py:624
  36.3 8.7 %collective-permute-start.7 = (f32[2,1024]{1,0:T(2,128)S(1)}, f32[2,1024]{1,0:T(2,128)S(1)}, u32[]{:S(2)}, u32[]{:S(2)}) collective-permute-start(f32[2,1024]{1,0:T(2,128)S(1)} %get-tuple-element.51), channel_id=1, source_target_pairs={{0,252},{4,8},{8,4},{12,16},{16,12},{20,24},{24,20},{28,32},{32,28... | collective-permute-start | bytes 24584 | tf_op jit(solution)/shard_map/ppermute | solution.py:625
  37.6 7.5 %collective-permute-start.8 = (f32[2,1024]{1,0:T(2,128)S(1)}, f32[2,1024]{1,0:T(2,128)S(1)}, u32[]{:S(2)}, u32[]{:S(2)}) collective-permute-start(f32[2,1024]{1,0:T(2,128)S(1)} %get-tuple-element.52), channel_id=1, source_target_pairs={{0,8},{4,12},{8,16},{12,20},{16,24},{20,28},{24,32},{28,36},{32,40... | collective-permute-start | bytes 24584 | tf_op jit(solution)/shard_map/ppermute | solution.py:54
  38.5 6.6 %collective-permute-start.9 = (f32[2,1024]{1,0:T(2,128)S(1)}, f32[2,1024]{1,0:T(2,128)S(1)}, u32[]{:S(2)}, u32[]{:S(2)}) collective-permute-start(f32[2,1024]{1,0:T(2,128)S(1)} %get-tuple-element.53), channel_id=1, source_target_pairs={{0,248},{4,252},{8,0},{12,4},{16,8},{20,12},{24,16},{28,20},{32,24... | collective-permute-start | bytes 24584 | tf_op jit(solution)/shard_map/ppermute | solution.py:54
  45.1 6.4 %collective-permute-start.12 = (bf16[112,512]{1,0:T(8,128)(2,1)S(1)}, bf16[112,512]{1,0:T(8,128)(2,1)S(1)}, u32[]{:S(2)}, u32[]{:S(2)}) collective-permute-start(bf16[112,512]{1,0:T(8,128)(2,1)S(1)} %merge.1.refs_0_), channel_id=1, source_target_pairs={{0,3},{1,0},{2,1},{3,2},{4,7},{5,4},{6,5},{7,6},{8,11},{9,8},{10,9... | collective-permute-start | bytes 344072 | tf_op jit(solution)/shard_map/ppermute | solution.py:54
  47.6 6.3 %collective-permute-start.11 = (bf16[112,512]{1,0:T(8,128)(2,1)S(1)}, bf16[112,512]{1,0:T(8,128)(2,1)S(1)}, u32[]{:S(2)}, u32[]{:S(2)}) collective-permute-start(bf16[112,512]{1,0:T(8,128)(2,1)S(1)} %merge.1.refs_0_), channel_id=1, source_target_pairs={{0,2},{1,3},{2,0},{3,1},{4,6},{5,7},{6,4},{7,5},{8,10},{9,11},{10,... | collective-permute-start | bytes 344072 | tf_op jit(solution)/shard_map/ppermute | solution.py:54
  48.8 6.4 %collective-permute-start.10 = (bf16[112,512]{1,0:T(8,128)(2,1)S(1)}, bf16[112,512]{1,0:T(8,128)(2,1)S(1)}, u32[]{:S(2)}, u32[]{:S(2)}) collective-permute-start(bf16[112,512]{1,0:T(8,128)(2,1)S(1)} %merge.1.refs_0_), channel_id=1, source_target_pairs={{0,1},{1,2},{2,3},{3,0},{4,5},{5,6},{6,7},{7,4},{8,9},{9,10},{10,1... | collective-permute-start | bytes 344072 | tf_op jit(solution)/shard_map/ppermute | solution.py:54

commit v2 on v1

--- a/solution.py
+++ b/solution.py
@@ -389,8 +389,8 @@
     sums_ref,
     conv_ref,
 ):
-    taps = conv_ref.shape[1]
-    channels = conv_ref.shape[2]
+    channels = conv_ref.shape[1]
+    taps = conv_ref.shape[2] // channels
     share = bounds_ref.shape[1]
     starts, ends, count, _, _ = share_bounds(where_ref, own_ref, left_ref, right_ref, last_seq, share, EDGE)
     bounds_ref[0] = jnp.broadcast_to(starts, (share, TILE))
@@ -398,7 +398,8 @@
     sums_ref[...] = jnp.zeros_like(sums_ref)
     for q in range(2):
         for k in range(taps):
-            conv_ref[q, k] = turned_ref[q, :, k * channels : (k + 1) * channels].T
+            at = (taps - 1 - k) * channels
+            conv_ref[q, :, at : at + channels] = turned_ref[q, :, k * channels : (k + 1) * channels].T
 
     def work(t, kept_ref, at):
         frames, _ = local_frames(t)
@@ -407,11 +408,7 @@
         )
         both = range(2)
         stacked = [with_neighbours(kept_ref[at, q, 1].astype(f32) * residual_ref[t, q : q + 1, :]) for q in both]
-        grad_hidden = [jnp.zeros((channels, TILE), f32) for q in both]
-        for k in range(taps):
-            for q in both:
-                part = stacked[q][(taps - 1 - k) * channels : (taps - k) * channels]
-                grad_hidden[q] = grad_hidden[q] + jnp.dot(conv_ref[q, k], part, preferred_element_type=f32)
+        grad_hidden = [jnp.dot(conv_ref[q], stacked[q], preferred_element_type=f32) for q in both]
         normed = [kept_ref[at, q, 0].astype(f32) for q in both]
         first_mean = [column_mean(x) for x in grad_hidden]
         second_mean = [column_mean(grad_hidden[q] * normed[q]) for q in both]
@@ -638,7 +635,7 @@
         scratch_shapes=[
             VMEM((2, share, TILE), f32),
             VMEM((taps * share, 2 * channels), f32),
-            VMEM(conv_second.shape, bf16),
+            VMEM(turned.shape, bf16),
         ],
     )(where, to_mate, left, right, residual, near, kept, turned)
 

time: 56.9 us -> 57 us (level)
  transfers between devices with their start and end apart: 14 -> 14, of which waited for: 7 -> 7; matrix products, arithmetic and copies ran while one was open for 0% -> 0% of each run, Pallas kernels for 15% -> 16%
where the time goes in v2:
time: 57 us; the launch traced here: 56.8 us
  starting transfers between devices  27.4 us (48%)
  waiting for transfers between devices  15.6 us (27%)
  Pallas kernels  12.9 us (23%)
  between operations  0.76 us (1%)
    ppermute x8, starting transfers between devices, rotate(): lax.ppermute(block, axis, [(i, (i + distance) % size) for i in range(size)])  15.4 us
    ppermute x8, waiting for transfers between devices, rotate(): lax.ppermute(block, axis, [(i, (i + distance) % size) for i in range(size)])  10.3 us
    ppermute x1, starting transfers between devices, body(): lax.ppermute(to_outer, 'seq', [(s, outer_of(s)) for s in range(seq_size)])  6.1 us
    ppermute x1, waiting for transfers between devices, body(): lax.ppermute(targets, ('seq', 'mp'), [((s + (-REACH if m % 2 == 0 else RE...  4.78 us
    all_to_all x1, starting transfers between devices, body(): everyone = lax.all_to_all(spread, 'seq', 0, 0, tiled=True)  4.59 us
    pallas_call x1, Pallas kernels, body(): call(functools.partial(forward_kernel, last_seq), 'forward', flops=2 * pe...  4.28 us
    pallas_call x1, Pallas kernels, body(): call(prepare_kernel, 'prepare', vmem=12, flops=2 * block * width * taps *...  2.39 us
    pallas_call x1, Pallas kernels, body(): call(functools.partial(backward_kernel, last_seq), 'backward', flops=2 *...  2.13 us
  transfers between devices with their start and end apart: 14, of which 7 were waited for; matrix products, arithmetic and copies ran while one was open for 0% of the time, Pallas kernels for 16%

profile of v2, /device:TPU:0, one launch (start us, length us, event | category | flops | bytes accessed | tf_op | source)
XLA Modules:
  0.0 56.8 jit_solution(5919119637997803954)
XLA Ops:
  0.6 0.1 pad_add_fusion.where_ref
  0.7 0.8 %pack.1 = (f32[8,1024]{1,0:T(8,128)S(1)}, f32[8,1024]{1,0:T(8,128)S(1)}) custom-call(s32[2]{0:T(128)S(1)} %pad_add_fusion.where_ref, s32[1,128]{1,0:T(1,128)} %bitcast.9, f32[2,1024]{1,0:T(2,128)} %targets_ref.1, bf16[2,256]{1,0:T(2,128)(2,1)} %readout_ref.1, bf16[128,1024]{1,0:T(8,128)(2,1)} %rows_ref.1, bf16[128,1024]{1,0:T(8,128)(2,1)} %rows_ref.1), custom_call_target="tpu_custom_call" | custom-call | bytes 65536 | tf_op jit(solution)/shard_map/pack/pallas_call | solution.py:504
  1.6 6.1 %collective-permute-start.1 = (f32[8,1024]{1,0:T(8,128)S(1)}, f32[8,1024]{1,0:T(8,128)S(1)}, u32[]{:S(2)}, u32[]{:S(2)}) collective-permute-start(f32[8,1024]{1,0:T(8,128)S(1)} %get-tuple-element.30), channel_id=1, source_target_pairs={{0,252},{4,8},{8,4},{12,16},{16,12},{20,24},{24,20},{28,32},{32,28... | collective-permute-start | bytes 98312 | tf_op jit(solution)/shard_map/ppermute | solution.py:525
  7.7 0.0 collective-permute-start
  7.7 0.0 collective-permute-start.2
  7.7 2.4 %prepare.1 = (s32[64,128]{1,0:T(8,128)}, bf16[384,128]{1,0:T(8,128)(2,1)S(1)}, bf16[1008,128]{1,0:T(8,128)(2,1)S(1)}, bf16[1008,128]{1,0:T(8,128)(2,1)S(1)}, bf1...) custom-call(s32[2]{0:T(128)S(1)} %pad_add_fusion.where_ref, ...), custom_call_target="tpu_custom_call" | custom-call | flops 100663296 | bytes 1835008 | tf_op jit(solution)/shard_map/prepare/pallas_call | solution.py:537
  10.1 4.8 %collective-permute-done.2.far_ref = f32[2,1024]{1,0:T(2,128)S(1)} collective-permute-done((f32[2,1024]{1,0:T(2,128)}, f32[2,1024]{1,0:T(2,128)S(1)}, u32[]{:S(2)}, u32[]{:S(2)}) %collective-permute-start.2) | collective-permute-done | bytes 8224 | tf_op jit(solution)/shard_map/ppermute | solution.py:526
  14.8 0.0 collective-permute-done.1.outer_ref
  14.9 0.0 collective-permute-done.mate_ref
  14.9 0.8 %pieces.1 = (bf16[1008,128]{1,0:T(8,128)(2,1)S(1)}, bf16[1008,128]{1,0:T(8,128)(2,1)S(1)}, bf16[1008,128]{1,0:T(8,128)(2,1)S(1)}, bf16[1008,128]{1,0:T(8,128)(2,...) custom-call(s32[2]{0:T(128)S(1)} %pad_add_fusion.where_ref, ...), custom_call_target="tpu_custom_call", output_to_operand_aliasing={{0}: (5, {}), {1}: (6, {}), {2}: (7, {}), {3}: (8, {})} | custom-call | flops 25165824 | bytes 786432 | tf_op jit(solution)/shard_map/pieces/pallas_call | solution.py:558
  15.7 0.1 collective-permute-start.3
  15.7 3.1 %collective-permute-start.4 = (bf16[1008,128]{1,0:T(8,128)(2,1)S(1)}, bf16[1008,128]{1,0:T(8,128)(2,1)S(1)}, u32[]{:S(2)}, u32[]{:S(2)}) collective-permute-start(bf16[1008,128]{1,0:T(8,128)(2,1)S(1)} %get-tuple-element.39), channel_id=1, source_target_pairs={{0,2},{1,3},{2,0},{3,1},{4,6},{5,7},{6,4},{7,5},{8,10},{9,11},{10,... | collective-permute-start | bytes 774152 | tf_op jit(solution)/shard_map/ppermute | solution.py:54
  18.9 2.5 %collective-permute-start.5 = (bf16[1008,128]{1,0:T(8,128)(2,1)S(1)}, bf16[1008,128]{1,0:T(8,128)(2,1)S(1)}, u32[]{:S(2)}, u32[]{:S(2)}) collective-permute-start(bf16[1008,128]{1,0:T(8,128)(2,1)S(1)} %get-tuple-element.40), channel_id=1, source_target_pairs={{0,3},{1,0},{2,1},{3,2},{4,7},{5,4},{6,5},{7,6},{8,11},{9,8},{10,9... | collective-permute-start | bytes 774152 | tf_op jit(solution)/shard_map/ppermute | solution.py:54
  21.4 4.6 %all-to-all-start = ((s32[64,1,128]{2,1,0:T(1,128)}), s32[64,1,128]{2,1,0:T(1,128)S(1)}, u32[]{:S(2)}, u32[]{:S(2)}) async-start(s32[64,1,128]{2,1,0:T(1,128)} %bitcast.8), calls=%async_computation | async-start | bytes 65536 | tf_op jit(solution)/shard_map/all_to_all | solution.py:572
  26.0 4.0 %collective-permute-done.4.two_ref.refs_6_ = bf16[1008,128]{1,0:T(8,128)(2,1)S(1)} collective-permute-done((bf16[1008,128]{1,0:T(8,128)(2,1)S(1)}, bf16[1008,128]{1,0:T(8,128)(2,1)S(1)}, u32[]{:S(2)}, u32[]{:S(2)}) %collective-permute-start.4) | collective-permute-done | bytes 258080 | tf_op jit(solution)/shard_map/ppermute | solution.py:54
  30.0 0.5 collective-permute-done.5.three_ref.refs_7_
  30.6 4.3 %forward.1 = (f32[3,2,512]{2,1,0:T(2,128)S(1)}, s32[2]{0:T(128)S(1)}, bf16[1,2,3,256,512]{4,3,2,1,0:T(8,128)(2,1)S(1)}, bf16[2,2,3,256,512]{4,3,2,1,0:T(8,128)(2,1)}) custom-call(s32[2]{0:T(128)S(1)} %pad_add_fusion.where_ref, f32[8,1024]{1,0:T(8,128)S(1)} %get-tuple-element.28.own_ref, f32[8,1024]{1,0:T(8,128)S(1)} %get-tuple-element.35.left_ref, ...), custom_call_target="tpu_custom_call" | custom-call | flops 1006632960 | bytes 3145728 | tf_op jit(solution)/shard_map/forward/pallas_call | solution.py:583
  34.9 0.6 all-to-all-done
  35.4 0.8 %align.1 = (f32[3,2,512]{2,1,0:T(2,128)S(1)}, bf16[2,2,3,256,512]{4,3,2,1,0:T(8,128)(2,1)S(1)}, f32[2,1024]{1,0:T(2,128)S(1)}, f32[2,1024]{1,0:T(2,128)S(1)}, f3...) custom-call(s32[2]{0:T(128)S(1)} %pad_add_fusion.where_ref, s32[2]{0:T(128)S(1)} %get-tuple-element.42.offset_ref, ...), custom_call_target="tpu_custom_call" | custom-call | bytes 98304 | tf_op jit(solution)/shard_map/align/pallas_call | solution.py:605
  36.2 0.1 collective-permute-start.6
  36.3 1.2 %collective-permute-start.7 = (f32[2,1024]{1,0:T(2,128)S(1)}, f32[2,1024]{1,0:T(2,128)S(1)}, u32[]{:S(2)}, u32[]{:S(2)}) collective-permute-start(f32[2,1024]{1,0:T(2,128)S(1)} %get-tuple-element.51), channel_id=1, source_target_pairs={{0,252},{4,8},{8,4},{12,16},{16,12},{20,24},{24,20},{28,32},{32,28... | collective-permute-start | bytes 24584 | tf_op jit(solution)/shard_map/ppermute | solution.py:622
  37.6 0.9 %collective-permute-start.8 = (f32[2,1024]{1,0:T(2,128)S(1)}, f32[2,1024]{1,0:T(2,128)S(1)}, u32[]{:S(2)}, u32[]{:S(2)}) collective-permute-start(f32[2,1024]{1,0:T(2,128)S(1)} %get-tuple-element.52), channel_id=1, source_target_pairs={{0,8},{4,12},{8,16},{12,20},{16,24},{20,28},{24,32},{28,36},{32,40... | collective-permute-start | bytes 24584 | tf_op jit(solution)/shard_map/ppermute | solution.py:54
  38.5 4.4 %collective-permute-start.9 = (f32[2,1024]{1,0:T(2,128)S(1)}, f32[2,1024]{1,0:T(2,128)S(1)}, u32[]{:S(2)}, u32[]{:S(2)}) collective-permute-start(f32[2,1024]{1,0:T(2,128)S(1)} %get-tuple-element.53), channel_id=1, source_target_pairs={{0,248},{4,252},{8,0},{12,4},{16,8},{20,12},{24,16},{28,20},{32,24... | collective-permute-start | bytes 24584 | tf_op jit(solution)/shard_map/ppermute | solution.py:54
  42.9 2.1 %backward.1.sums_ref = bf16[96,512]{1,0:T(8,128)(2,1)S(1)} custom-call(s32[2]{0:T(128)S(1)} %pad_add_fusion.where_ref, f32[8,1024]{1,0:T(8,128)S(1)} %get-tuple-element.28.own_ref, f32[8,1024]{1,0:T(8,128)S(1)} %get-tuple-element.35.left_ref, f32[8,1024]{1,0:T(8,128)S(1)} %get-tuple-element.36.right_ref, f32[3,2,512]{2,1,0:T(2,128)S(1)} %get-tuple-element.46.residual_ref, ...), custom_call_target="tpu_custom_call" | custom-call | flops 905969664 | bytes 3145728 | tf_op jit(solution)/shard_map/backward/pallas_call | solution.py:627
  45.0 0.0 collective-permute-done.6.refs_0_
  45.1 2.5 %collective-permute-start.12 = (bf16[112,512]{1,0:T(8,128)(2,1)S(1)}, bf16[112,512]{1,0:T(8,128)(2,1)S(1)}, u32[]{:S(2)}, u32[]{:S(2)}) collective-permute-start(bf16[112,512]{1,0:T(8,128)(2,1)S(1)} %merge.1.refs_0_), channel_id=1, source_target_pairs={{0,3},{1,0},{2,1},{3,2},{4,7},{5,4},{6,5},{7,6},{8,11},{9,8},{10,9... | collective-permute-start | bytes 344072 | tf_op jit(solution)/shard_map/ppermute | solution.py:54
  47.7 1.1 %collective-permute-start.11 = (bf16[112,512]{1,0:T(8,128)(2,1)S(1)}, bf16[112,512]{1,0:T(8,128)(2,1)S(1)}, u32[]{:S(2)}, u32[]{:S(2)}) collective-permute-start(bf16[112,512]{1,0:T(8,128)(2,1)S(1)} %merge.1.refs_0_), channel_id=1, source_target_pairs={{0,2},{1,3},{2,0},{3,1},{4,6},{5,7},{6,4},{7,5},{8,10},{9,11},{10,... | collective-permute-start | bytes 344072 | tf_op jit(solution)/shard_map/ppermute | solution.py:54
  48.8 0.7 %collective-permute-start.10 = (bf16[112,512]{1,0:T(8,128)(2,1)S(1)}, bf16[112,512]{1,0:T(8,128)(2,1)S(1)}, u32[]{:S(2)}, u32[]{:S(2)}) collective-permute-start(bf16[112,512]{1,0:T(8,128)(2,1)S(1)} %merge.1.refs_0_), channel_id=1, source_target_pairs={{0,1},{1,2},{2,3},{3,0},{4,5},{5,6},{6,7},{7,4},{8,9},{9,10},{10,1... | collective-permute-start | bytes 344072 | tf_op jit(solution)/shard_map/ppermute | solution.py:54
  49.5 2.1 %collective-permute-done.12.refs_3_ = bf16[112,512]{1,0:T(8,128)(2,1)S(1)} collective-permute-done((bf16[112,512]{1,0:T(8,128)(2,1)S(1)}, bf16[112,512]{1,0:T(8,128)(2,1)S(1)}, u32[]{:S(2)}, u32[]{:S(2)}) %collective-permute-start.12) | collective-permute-done | bytes 114720 | tf_op jit(solution)/shard_map/ppermute | solution.py:54
  51.5 2.5 %collective-permute-done.11.refs_2_ = bf16[112,512]{1,0:T(8,128)(2,1)S(1)} collective-permute-done((bf16[112,512]{1,0:T(8,128)(2,1)S(1)}, bf16[112,512]{1,0:T(8,128)(2,1)S(1)}, u32[]{:S(2)}, u32[]{:S(2)}) %collective-permute-start.11) | collective-permute-done | bytes 114720 | tf_op jit(solution)/shard_map/ppermute | solution.py:54
  54.0 1.2 %collective-permute-done.10.refs_1_ = bf16[112,512]{1,0:T(8,128)(2,1)S(1)} collective-permute-done((bf16[112,512]{1,0:T(8,128)(2,1)S(1)}, bf16[112,512]{1,0:T(8,128)(2,1)S(1)}, u32[]{:S(2)}, u32[]{:S(2)}) %collective-permute-start.10) | collective-permute-done | bytes 114720 | tf_op jit(solution)/shard_map/ppermute | solution.py:54
  55.2 1.6 %finish.1 = (f32[2,1024]{1,0:T(2,128)}, bf16[128,256]{1,0:T(8,128)(2,1)}) custom-call(s32[2]{0:T(128)S(1)} %pad_add_fusion.where_ref, bf16[112,512]{1,0:T(8,128)(2,1)S(1)} %merge.1.refs_0_, bf16[112,512]{1,0:T(8,128)(2,1)S(1)} %collective-permute-done.10.refs_1_, bf16[112,512]{1,0:T(8,128)(2,1)S(1)} %collective-permute-done.11.refs_2_, ...), custom_call_target="tpu_custom_call" | custom-call | flops 100663296 | bytes 786432 | tf_op jit(solution)/shard_map/finish/pallas_call | solution.py:653
  (5 shorter events, 0.1 us)
Async XLA Ops:
  1.6 13.3 %collective-permute-start.1 = (f32[8,1024]{1,0:T(8,128)S(1)}, f32[8,1024]{1,0:T(8,128)S(1)}, u32[]{:S(2)}, u32[]{:S(2)}) collective-permute-start(f32[8,1024]{1,0:T(8,128)S(1)} %get-tuple-element.30), channel_id=1, source_target_pairs={{0,252},{4,8},{8,4},{12,16},{16,12},{20,24},{24,20},{28,32},{32,28... | collective-permute-start | bytes 98312 | tf_op jit(solution)/shard_map/ppermute | solution.py:525
  7.7 7.2 %collective-permute-start = (f32[8,1024]{1,0:T(8,128)S(1)}, f32[8,1024]{1,0:T(8,128)S(1)}, u32[]{:S(2)}, u32[]{:S(2)}) collective-permute-start(f32[8,1024]{1,0:T(8,128)S(1)} %get-tuple-element.28.own_ref), channel_id=1, source_target_pairs={{0,4},{4,0},{8,12},{12,8},{16,20},{20,16},{24,28},{28,24},{32,36},... | collective-permute-start | bytes 98312 | tf_op jit(solution)/shard_map/ppermute | solution.py:524
  7.7 7.2 %collective-permute-start.2 = (f32[2,1024]{1,0:T(2,128)}, f32[2,1024]{1,0:T(2,128)S(1)}, u32[]{:S(2)}, u32[]{:S(2)}) collective-permute-start(f32[2,1024]{1,0:T(2,128)} %targets_ref.1), channel_id=1, source_target_pairs={{248,0},{9,1},{250,2},{11,3},{252,4},{13,5},{254,6},{15,7},{0,8},{... | collective-permute-start | bytes 24584 | tf_op jit(solution)/shard_map/ppermute | solution.py:526
  15.7 10.3 %collective-permute-start.3 = (bf16[1008,128]{1,0:T(8,128)(2,1)S(1)}, bf16[1008,128]{1,0:T(8,128)(2,1)S(1)}, u32[]{:S(2)}, u32[]{:S(2)}) collective-permute-start(bf16[1008,128]{1,0:T(8,128)(2,1)S(1)} %get-tuple-element.38), channel_id=1, source_target_pairs={{0,1},{1,2},{2,3},{3,0},{4,5},{5,6},{6,7},{7,4},{8,9},{9,10},{10,1... | collective-permute-start | bytes 774152 | tf_op jit(solution)/shard_map/ppermute | solution.py:54
  15.7 14.3 %collective-permute-start.4 = (bf16[1008,128]{1,0:T(8,128)(2,1)S(1)}, bf16[1008,128]{1,0:T(8,128)(2,1)S(1)}, u32[]{:S(2)}, u32[]{:S(2)}) collective-permute-start(bf16[1008,128]{1,0:T(8,128)(2,1)S(1)} %get-tuple-element.39), channel_id=1, source_target_pairs={{0,2},{1,3},{2,0},{3,1},{4,6},{5,7},{6,4},{7,5},{8,10},{9,11},{10,... | collective-permute-start | bytes 774152 | tf_op jit(solution)/shard_map/ppermute | solution.py:54
  18.9 11.7 %collective-permute-start.5 = (bf16[1008,128]{1,0:T(8,128)(2,1)S(1)}, bf16[1008,128]{1,0:T(8,128)(2,1)S(1)}, u32[]{:S(2)}, u32[]{:S(2)}) collective-permute-start(bf16[1008,128]{1,0:T(8,128)(2,1)S(1)} %get-tuple-element.40), channel_id=1, source_target_pairs={{0,3},{1,0},{2,1},{3,2},{4,7},{5,4},{6,5},{7,6},{8,11},{9,8},{10,9... | collective-permute-start | bytes 774152 | tf_op jit(solution)/shard_map/ppermute | solution.py:54
  21.4 14.0 %all-to-all-start = ((s32[64,1,128]{2,1,0:T(1,128)}), s32[64,1,128]{2,1,0:T(1,128)S(1)}, u32[]{:S(2)}, u32[]{:S(2)}) async-start(s32[64,1,128]{2,1,0:T(1,128)} %bitcast.8), calls=%async_computation | async-start | bytes 65536 | tf_op jit(solution)/shard_map/all_to_all | solution.py:572
  36.2 8.8 %collective-permute-start.6 = (f32[2,1024]{1,0:T(2,128)S(1)}, f32[2,1024]{1,0:T(2,128)S(1)}, u32[]{:S(2)}, u32[]{:S(2)}) collective-permute-start(f32[2,1024]{1,0:T(2,128)S(1)} %get-tuple-element.50), channel_id=1, source_target_pairs={{0,4},{4,0},{8,12},{12,8},{16,20},{20,16},{24,28},{28,24},{32,36},... | collective-permute-start | bytes 24584 | tf_op jit(solution)/shard_map/ppermute | solution.py:621
  36.3 8.7 %collective-permute-start.7 = (f32[2,1024]{1,0:T(2,128)S(1)}, f32[2,1024]{1,0:T(2,128)S(1)}, u32[]{:S(2)}, u32[]{:S(2)}) collective-permute-start(f32[2,1024]{1,0:T(2,128)S(1)} %get-tuple-element.51), channel_id=1, source_target_pairs={{0,252},{4,8},{8,4},{12,16},{16,12},{20,24},{24,20},{28,32},{32,28... | collective-permute-start | bytes 24584 | tf_op jit(solution)/shard_map/ppermute | solution.py:622
  37.6 7.5 %collective-permute-start.8 = (f32[2,1024]{1,0:T(2,128)S(1)}, f32[2,1024]{1,0:T(2,128)S(1)}, u32[]{:S(2)}, u32[]{:S(2)}) collective-permute-start(f32[2,1024]{1,0:T(2,128)S(1)} %get-tuple-element.52), channel_id=1, source_target_pairs={{0,8},{4,12},{8,16},{12,20},{16,24},{20,28},{24,32},{28,36},{32,40... | collective-permute-start | bytes 24584 | tf_op jit(solution)/shard_map/ppermute | solution.py:54
  38.5 6.6 %collective-permute-start.9 = (f32[2,1024]{1,0:T(2,128)S(1)}, f32[2,1024]{1,0:T(2,128)S(1)}, u32[]{:S(2)}, u32[]{:S(2)}) collective-permute-start(f32[2,1024]{1,0:T(2,128)S(1)} %get-tuple-element.53), channel_id=1, source_target_pairs={{0,248},{4,252},{8,0},{12,4},{16,8},{20,12},{24,16},{28,20},{32,24... | collective-permute-start | bytes 24584 | tf_op jit(solution)/shard_map/ppermute | solution.py:54
  45.1 6.4 %collective-permute-start.12 = (bf16[112,512]{1,0:T(8,128)(2,1)S(1)}, bf16[112,512]{1,0:T(8,128)(2,1)S(1)}, u32[]{:S(2)}, u32[]{:S(2)}) collective-permute-start(bf16[112,512]{1,0:T(8,128)(2,1)S(1)} %merge.1.refs_0_), channel_id=1, source_target_pairs={{0,3},{1,0},{2,1},{3,2},{4,7},{5,4},{6,5},{7,6},{8,11},{9,8},{10,9... | collective-permute-start | bytes 344072 | tf_op jit(solution)/shard_map/ppermute | solution.py:54
  47.7 6.3 %collective-permute-start.11 = (bf16[112,512]{1,0:T(8,128)(2,1)S(1)}, bf16[112,512]{1,0:T(8,128)(2,1)S(1)}, u32[]{:S(2)}, u32[]{:S(2)}) collective-permute-start(bf16[112,512]{1,0:T(8,128)(2,1)S(1)} %merge.1.refs_0_), channel_id=1, source_target_pairs={{0,2},{1,3},{2,0},{3,1},{4,6},{5,7},{6,4},{7,5},{8,10},{9,11},{10,... | collective-permute-start | bytes 344072 | tf_op jit(solution)/shard_map/ppermute | solution.py:54
  48.8 6.4 %collective-permute-start.10 = (bf16[112,512]{1,0:T(8,128)(2,1)S(1)}, bf16[112,512]{1,0:T(8,128)(2,1)S(1)}, u32[]{:S(2)}, u32[]{:S(2)}) collective-permute-start(bf16[112,512]{1,0:T(8,128)(2,1)S(1)} %merge.1.refs_0_), channel_id=1, source_target_pairs={{0,1},{1,2},{2,3},{3,0},{4,5},{5,6},{6,7},{7,4},{8,9},{9,10},{10,1... | collective-permute-start | bytes 344072 | tf_op jit(solution)/shard_map/ppermute | solution.py:54
